TPU v7x, 32 devices: a whole 2x2x4 slice. The times are simulated.
32 devices in a mesh: batch: 2 (over core), seq: 8 (over z, x), tensor: 2 (over y).
Axes of the slice: x: 2, y: 2, z: 4, core: 2. Of those that a mesh axis runs over, the one named last changes fastest.
Arguments:
- hidden: bfloat16 [2, 4096, 1536], P('batch', 'seq'), may hold values from -6 to 6
- lengths: int32 [2, 7], P('batch'), may hold values from 1 to 2048, as said below
- norm_attn: bfloat16 [1536], P(('batch', 'seq')), may hold values from 0.5 to 1.5
- w_query: bfloat16 [1536, 1536], P(('batch', 'seq'), 'tensor'), may hold values from -0.15625 to 0.15625
- key_weight_matrix: bfloat16 [1536, 256], P(('batch', 'seq'), 'tensor'), may hold values from -0.15625 to 0.15625
- value_weight_matrix: bfloat16 [1536, 256], P(('batch', 'seq'), 'tensor'), may hold values from -0.15625 to 0.15625
- b_query: bfloat16 [12, 128], P('tensor', ('batch', 'seq')), may hold values from -3 to 3
- key_bias_rows: bfloat16 [2, 128], P('tensor', ('batch', 'seq')), may hold values from -3 to 3
- value_bias_rows: bfloat16 [2, 128], P('tensor', ('batch', 'seq')), may hold values from -3 to 3
- w_out: bfloat16 [1536, 1536], P('tensor', ('batch', 'seq')), may hold values from -1.5 to 1.5
- norm_mlp: bfloat16 [1536], P(('batch', 'seq')), may hold values from 0.5 to 1.5
- w_gate: bfloat16 [1536, 8960], P(('batch', 'seq'), 'tensor'), may hold values from -0.15625 to 0.15625
- w_up: bfloat16 [1536, 8960], P(('batch', 'seq'), 'tensor'), may hold values from -0.15625 to 0.15625
- w_down: bfloat16 [8960, 1536], P('tensor', ('batch', 'seq')), may hold values from -0.0625 to 0.0625
- cotangent: bfloat16 [2, 4096, 1536], P('batch', 'seq'), may hold values from -6 to 6
Outputs:
- output: bfloat16 [2, 4096, 1536], P('batch', 'seq')
- grad_hidden: float32 [2, 4096, 1536], P('batch', 'seq')
- grad_norm_attn: float32 [1536], P(('batch', 'seq'))
- grad_query: float32 [1536, 1536], P(('batch', 'seq'), 'tensor')
- grad_key: float32 [1536, 256], P(('batch', 'seq'), 'tensor')
- grad_value: float32 [1536, 256], P(('batch', 'seq'), 'tensor')
- grad_bias_query: float32 [12, 128], P('tensor', ('batch', 'seq'))
- grad_bias_key: float32 [2, 128], P('tensor', ('batch', 'seq'))
- grad_bias_value: float32 [2, 128], P('tensor', ('batch', 'seq'))
- grad_out: float32 [1536, 1536], P('tensor', ('batch', 'seq'))
- grad_norm_mlp: float32 [1536], P(('batch', 'seq'))
- grad_gate: float32 [1536, 8960], P(('batch', 'seq'), 'tensor')
- grad_up: float32 [1536, 8960], P(('batch', 'seq'), 'tensor')
- grad_down: float32 [8960, 1536], P('tensor', ('batch', 'seq'))
Inputs may be any that keep to these rules, and one draw needn't show every extreme that they name: In each row the 7 lengths sum to 4096, and the first or the last of them is 2048.
All inputs are finite; a program needn't handle non-finite values.
Results may differ from a plain program's by a relative error of at most 0.03.
Values may be sent and summed in bfloat16 or wider, within the bound.
A program may use at most 256 MiB of HBM per device.

v0:
```python
import jax
import jax.numpy as jnp
from jax import lax
from jax.sharding import PartitionSpec as P

HEAD_SIZE = 128


NORM_EPS = 1e-06
ROPE_BASE = 10000.0
MASKED = -1e30


def row_positions(stored, shards, half_rows):
    slot_id = stored // half_rows
    inner = stored % half_rows
    shard_id = slot_id // 2
    row_block = jnp.where(slot_id % 2 == 0, shard_id, 2 * shards - 1 - shard_id)
    return row_block * half_rows + inner


def doc_info(row_pos, doc_lengths):
    doc_ends = jnp.cumsum(doc_lengths)
    doc_starts = doc_ends - doc_lengths
    inside = (row_pos[:, None] >= doc_starts[None, :]) & (row_pos[:, None] < doc_ends[None, :])
    doc_ids = jnp.sum(jnp.where(row_pos[:, None] >= doc_ends[None, :], 1, 0), axis=1).astype(
        jnp.int32
    )
    offsets = jnp.sum(jnp.where(inside, doc_starts[None, :], 0), axis=1)
    return (doc_ids, row_pos - offsets)


def rotary(doc_pos, head_dim):
    half_dim = head_dim // 2
    freqs = ROPE_BASE ** (-2.0 * jnp.arange(half_dim, dtype=jnp.float32) / head_dim)
    angles = doc_pos.astype(jnp.float32)[:, None] * freqs[None, :]
    return (jnp.cos(angles), jnp.sin(angles))


def turn(values, cosine_table, sine_table):
    half_dim = values.shape[-1] // 2
    first_half = values[..., :half_dim]
    second_half = values[..., half_dim:]
    cos_b = cosine_table[:, None, :]
    sin_b = sine_table[:, None, :]
    return jnp.concatenate(
        [first_half * cos_b - second_half * sin_b, second_half * cos_b + first_half * sin_b],
        axis=-1,
    )


def turn_back(values, cosine_table, sine_table):
    half_dim = values.shape[-1] // 2
    first_half = values[..., :half_dim]
    second_half = values[..., half_dim:]
    cos_b = cosine_table[:, None, :]
    sin_b = sine_table[:, None, :]
    return jnp.concatenate(
        [first_half * cos_b + second_half * sin_b, second_half * cos_b - first_half * sin_b],
        axis=-1,
    )


def norm_forward(resid, gain):
    factor = lax.rsqrt(jnp.mean(resid * resid, axis=-1, keepdims=True) + NORM_EPS)
    return (resid * factor * gain, factor)


def norm_backward(resid, factor, gain, grad_in):
    weighted = grad_in * gain
    grad_resid = factor * weighted - resid * factor**3 * jnp.mean(
        weighted * resid, axis=-1, keepdims=True
    )
    grad_gain = jnp.sum(grad_in * resid * factor, axis=0)
    return (grad_resid, grad_gain)


def key_mask(q_rows, q_docs, stored, shards, half_rows, doc_lengths):
    k_rows = row_positions(stored, shards, half_rows)
    k_docs, unused = doc_info(k_rows, doc_lengths)
    return (q_docs[:, None] == k_docs[None, :]) & (k_rows[None, :] <= q_rows[:, None])


def fold_block(carried, query_rows, key_blk, val_blk, allowed, softmax_scale):
    run_max, run_sum, run_acc = carried

    def fold_work(unused):
        scores = (
            jnp.einsum("qhd,kd->hqk", query_rows, key_blk, preferred_element_type=jnp.float32)
            * softmax_scale
        )
        scores = jnp.where(allowed[None], scores, MASKED)
        new_max = jnp.maximum(run_max, jnp.max(scores, axis=-1))
        weights = jnp.where(allowed[None], jnp.exp(scores - new_max[..., None]), 0.0)
        shrink = jnp.exp(run_max - new_max)
        new_sum = run_sum * shrink + jnp.sum(weights, axis=-1)
        new_acc = run_acc * shrink[..., None] + jnp.einsum(
            "hqk,kd->hqd", weights.astype(jnp.bfloat16), val_blk, preferred_element_type=jnp.float32
        )
        return (new_max, new_sum, new_acc)

    def fold_skip(unused):
        return (run_max, run_sum, run_acc)

    return lax.cond(jnp.any(allowed), fold_work, fold_skip, None)


def attend_piece(
    carried,
    query_rows,
    q_rows,
    q_docs,
    key_heads_full,
    value_heads_full,
    doc_lengths,
    shards,
    half_rows,
    softmax_scale,
):
    row_count = key_heads_full.shape[0]
    tok_count = query_rows.shape[0]
    key_step = 2 * tok_count
    blocks = row_count // key_step

    def attend_one(state_now, inputs):
        key_blk, val_blk, block_index = inputs
        stored = block_index * key_step + jnp.arange(key_step, dtype=jnp.int32)
        allowed = key_mask(q_rows, q_docs, stored, shards, half_rows, doc_lengths)
        return (fold_block(state_now, query_rows, key_blk, val_blk, allowed, softmax_scale), None)

    stacked = (
        key_heads_full.reshape(blocks, key_step, key_heads_full.shape[1]),
        value_heads_full.reshape(blocks, key_step, value_heads_full.shape[1]),
        jnp.arange(blocks, dtype=jnp.int32),
    )
    state_end, unused = lax.scan(attend_one, carried, stacked)
    return state_end


def grad_keys(
    query_rows,
    q_rows,
    q_docs,
    key_heads_full,
    value_heads_full,
    log_total,
    d_out,
    row_dot,
    doc_lengths,
    shards,
    half_rows,
    softmax_scale,
):
    row_count = key_heads_full.shape[0]
    tok_count = query_rows.shape[0]
    head_dim = key_heads_full.shape[1]
    key_step = 2 * tok_count
    blocks = row_count // key_step

    def grad_one(grad_q, inputs):
        key_blk, val_blk, block_index = inputs
        stored = block_index * key_step + jnp.arange(key_step, dtype=jnp.int32)
        allowed = key_mask(q_rows, q_docs, stored, shards, half_rows, doc_lengths)

        def one_work(unused):
            scores = (
                jnp.einsum("qhd,kd->hqk", query_rows, key_blk, preferred_element_type=jnp.float32)
                * softmax_scale
            )
            probs = jnp.where(allowed[None], jnp.exp(scores - log_total[..., None]), 0.0)
            grad_v = jnp.einsum(
                "hqk,qhd->kd", probs.astype(jnp.bfloat16), d_out, preferred_element_type=jnp.float32
            )
            grad_p = jnp.einsum("qhd,kd->hqk", d_out, val_blk, preferred_element_type=jnp.float32)
            grad_s = (probs * (grad_p - row_dot[..., None])).astype(jnp.bfloat16)
            add_q = (
                jnp.einsum("hqk,kd->qhd", grad_s, key_blk, preferred_element_type=jnp.float32)
                * softmax_scale
            )
            grad_k = (
                jnp.einsum("hqk,qhd->kd", grad_s, query_rows, preferred_element_type=jnp.float32)
                * softmax_scale
            )
            return (grad_q + add_q, grad_k, grad_v)

        def one_skip(unused):
            empty = jnp.zeros((key_step, head_dim), jnp.float32)
            return (grad_q, empty, empty)

        new_q, grad_k, grad_v = lax.cond(jnp.any(allowed), one_work, one_skip, None)
        return (new_q, (grad_k, grad_v))

    stacked = (
        key_heads_full.reshape(blocks, key_step, head_dim),
        value_heads_full.reshape(blocks, key_step, head_dim),
        jnp.arange(blocks, dtype=jnp.int32),
    )
    start_q = jnp.zeros(query_rows.shape, jnp.float32)
    grad_q, (grad_k, grad_v) = lax.scan(grad_one, start_q, stacked)
    return (grad_q, grad_k.reshape(row_count, head_dim), grad_v.reshape(row_count, head_dim))


def on_device(
    hidden,
    lengths,
    norm_attn,
    w_query,
    key_weight_matrix,
    value_weight_matrix,
    b_query,
    key_bias_rows,
    value_bias_rows,
    w_out,
    norm_mlp,
    w_gate,
    w_up,
    w_down,
    cotangent,
):
    shards = lax.axis_size("seq")
    tok_count = hidden.shape[1]
    half_rows = tok_count // 2
    doc_lengths = lengths[0]
    stored = lax.axis_index("seq") * tok_count + jnp.arange(tok_count, dtype=jnp.int32)
    q_rows = row_positions(stored, shards, half_rows)
    q_docs, doc_pos = doc_info(q_rows, doc_lengths)
    cosine_table, sine_table = rotary(doc_pos, HEAD_SIZE)
    softmax_scale = HEAD_SIZE ** (-0.5)
    (
        n_attn,
        wq_all,
        wk_all,
        wv_all,
        bq_all,
        bk_all,
        bv_all,
        wo_all,
        n_mlp,
        wg_all,
        wu_all,
        wd_all,
    ) = (
        lax.all_gather(norm_attn, ("batch", "seq"), axis=0, tiled=True),
        lax.all_gather(w_query, ("batch", "seq"), axis=0, tiled=True),
        lax.all_gather(key_weight_matrix, ("batch", "seq"), axis=0, tiled=True),
        lax.all_gather(value_weight_matrix, ("batch", "seq"), axis=0, tiled=True),
        lax.all_gather(b_query, ("batch", "seq"), axis=1, tiled=True),
        lax.all_gather(key_bias_rows, ("batch", "seq"), axis=1, tiled=True),
        lax.all_gather(value_bias_rows, ("batch", "seq"), axis=1, tiled=True),
        lax.all_gather(w_out, ("batch", "seq"), axis=1, tiled=True),
        lax.all_gather(norm_mlp, ("batch", "seq"), axis=0, tiled=True),
        lax.all_gather(w_gate, ("batch", "seq"), axis=0, tiled=True),
        lax.all_gather(w_up, ("batch", "seq"), axis=0, tiled=True),
        lax.all_gather(w_down, ("batch", "seq"), axis=1, tiled=True),
    )
    heads = wq_all.shape[1] // HEAD_SIZE
    resid = hidden[0].astype(jnp.float32)
    gain_attn = n_attn.astype(jnp.float32)
    normed1, factor1 = norm_forward(resid, gain_attn)
    h_first = normed1.astype(jnp.bfloat16)
    query_linear = jnp.dot(h_first, wq_all, preferred_element_type=jnp.float32) + bq_all.reshape(
        -1
    ).astype(jnp.float32)
    key_linear = jnp.dot(h_first, wk_all, preferred_element_type=jnp.float32) + bk_all.reshape(
        -1
    ).astype(jnp.float32)
    value_linear = jnp.dot(h_first, wv_all, preferred_element_type=jnp.float32) + bv_all.reshape(
        -1
    ).astype(jnp.float32)
    query_rows = turn(
        query_linear.reshape(tok_count, heads, HEAD_SIZE), cosine_table, sine_table
    ).astype(jnp.bfloat16)
    key_rot = (
        turn(key_linear.reshape(tok_count, 1, HEAD_SIZE), cosine_table, sine_table)
        .reshape(tok_count, HEAD_SIZE)
        .astype(jnp.bfloat16)
    )
    val_rot = value_linear.astype(jnp.bfloat16)
    initial = (
        jnp.full((heads, tok_count), MASKED, jnp.float32),
        jnp.zeros((heads, tok_count), jnp.float32),
        jnp.zeros((heads, tok_count, HEAD_SIZE), jnp.float32),
    )
    run_max, run_sum, run_acc = attend_piece(
        initial,
        query_rows,
        q_rows,
        q_docs,
        lax.all_gather(key_rot, "seq", axis=0, tiled=True),
        lax.all_gather(val_rot, "seq", axis=0, tiled=True),
        doc_lengths,
        shards,
        half_rows,
        softmax_scale,
    )
    out_full = jnp.transpose(run_acc / run_sum[..., None], (1, 0, 2))
    log_total = run_max + jnp.log(run_sum)
    out_low = out_full.reshape(tok_count, heads * HEAD_SIZE).astype(jnp.bfloat16)
    attn_branch = lax.psum(
        jnp.dot(out_low, wo_all, preferred_element_type=jnp.float32).astype(jnp.bfloat16), "tensor"
    ).astype(jnp.float32)
    mid_resid = resid + attn_branch
    gain_mlp = n_mlp.astype(jnp.float32)
    normed2, factor2 = norm_forward(mid_resid, gain_mlp)
    h_second = normed2.astype(jnp.bfloat16)
    gate_lin = jnp.dot(h_second, wg_all, preferred_element_type=jnp.float32)
    up_lin = jnp.dot(h_second, wu_all, preferred_element_type=jnp.float32)
    sig_val = jax.nn.sigmoid(gate_lin)
    silu_out = gate_lin * sig_val
    hidden_mid = (silu_out * up_lin).astype(jnp.bfloat16)
    mlp_branch = lax.psum(
        jnp.dot(hidden_mid, wd_all, preferred_element_type=jnp.float32).astype(jnp.bfloat16),
        "tensor",
    ).astype(jnp.float32)
    output = (mid_resid + mlp_branch).astype(jnp.bfloat16)
    grad_y = cotangent[0]
    d_hidden_mid = jnp.dot(grad_y, wd_all.T, preferred_element_type=jnp.float32)
    g_down = jnp.dot(hidden_mid.T, grad_y, preferred_element_type=jnp.float32)
    d_gate = (d_hidden_mid * up_lin * sig_val * (1.0 + gate_lin * (1.0 - sig_val))).astype(
        jnp.bfloat16
    )
    d_up = (d_hidden_mid * silu_out).astype(jnp.bfloat16)
    g_gate = jnp.dot(h_second.T, d_gate, preferred_element_type=jnp.float32)
    g_up = jnp.dot(h_second.T, d_up, preferred_element_type=jnp.float32)
    d_h_second = lax.psum(
        (
            jnp.dot(d_gate, wg_all.T, preferred_element_type=jnp.float32)
            + jnp.dot(d_up, wu_all.T, preferred_element_type=jnp.float32)
        ).astype(jnp.bfloat16),
        "tensor",
    ).astype(jnp.float32)
    d_mid_norm, g_norm_mlp = norm_backward(mid_resid, factor2, gain_mlp, d_h_second)
    d_mid = grad_y.astype(jnp.float32) + d_mid_norm
    d_attn = d_mid.astype(jnp.bfloat16)
    g_out = jnp.dot(out_low.T, d_attn, preferred_element_type=jnp.float32)
    d_out = (
        jnp.dot(d_attn, wo_all.T, preferred_element_type=jnp.float32)
        .reshape(tok_count, heads, HEAD_SIZE)
        .astype(jnp.bfloat16)
    )
    row_dot = jnp.einsum("qhd,qhd->hq", d_out.astype(jnp.float32), out_full)
    key_whole, val_whole = (
        lax.all_gather(key_rot, "seq", axis=0, tiled=True),
        lax.all_gather(val_rot, "seq", axis=0, tiled=True),
    )
    grad_q, grad_k_all, grad_v_all = grad_keys(
        query_rows,
        q_rows,
        q_docs,
        key_whole,
        val_whole,
        log_total,
        d_out,
        row_dot,
        doc_lengths,
        shards,
        half_rows,
        softmax_scale,
    )
    grad_k, grad_v = (
        lax.psum_scatter(
            grad_k_all.astype(jnp.bfloat16), "seq", scatter_dimension=0, tiled=True
        ).astype(jnp.float32),
        lax.psum_scatter(
            grad_v_all.astype(jnp.bfloat16), "seq", scatter_dimension=0, tiled=True
        ).astype(jnp.float32),
    )
    dq_lin = (
        turn_back(grad_q, cosine_table, sine_table)
        .reshape(tok_count, heads * HEAD_SIZE)
        .astype(jnp.bfloat16)
    )
    dk_lin = (
        turn_back(grad_k.reshape(tok_count, 1, HEAD_SIZE), cosine_table, sine_table)
        .reshape(tok_count, HEAD_SIZE)
        .astype(jnp.bfloat16)
    )
    dv_lin = grad_v.astype(jnp.bfloat16)
    g_query = jnp.dot(h_first.T, dq_lin, preferred_element_type=jnp.float32)
    g_key = jnp.dot(h_first.T, dk_lin, preferred_element_type=jnp.float32)
    g_value = jnp.dot(h_first.T, dv_lin, preferred_element_type=jnp.float32)
    g_bias_q = jnp.sum(dq_lin.astype(jnp.float32), axis=0).reshape(heads, HEAD_SIZE)
    g_bias_k = jnp.sum(dk_lin.astype(jnp.float32), axis=0).reshape(1, HEAD_SIZE)
    g_bias_v = jnp.sum(dv_lin.astype(jnp.float32), axis=0).reshape(1, HEAD_SIZE)
    d_h_first = lax.psum(
        (
            jnp.dot(dq_lin, wq_all.T, preferred_element_type=jnp.float32)
            + jnp.dot(dk_lin, wk_all.T, preferred_element_type=jnp.float32)
            + jnp.dot(dv_lin, wv_all.T, preferred_element_type=jnp.float32)
        ).astype(jnp.bfloat16),
        "tensor",
    ).astype(jnp.float32)
    d_resid_norm, g_norm_attn = norm_backward(resid, factor1, gain_attn, d_h_first)
    d_hidden = d_mid + d_resid_norm
    (
        s_norm_attn,
        s_query,
        s_key,
        s_value,
        s_bias_q,
        s_bias_k,
        s_bias_v,
        s_out,
        s_norm_mlp,
        s_gate,
        s_up,
        s_down,
    ) = (
        lax.psum_scatter(g_norm_attn, ("batch", "seq"), scatter_dimension=0, tiled=True),
        lax.psum_scatter(g_query, ("batch", "seq"), scatter_dimension=0, tiled=True),
        lax.psum_scatter(g_key, ("batch", "seq"), scatter_dimension=0, tiled=True),
        lax.psum_scatter(g_value, ("batch", "seq"), scatter_dimension=0, tiled=True),
        lax.psum_scatter(g_bias_q, ("batch", "seq"), scatter_dimension=1, tiled=True),
        lax.psum_scatter(g_bias_k, ("batch", "seq"), scatter_dimension=1, tiled=True),
        lax.psum_scatter(g_bias_v, ("batch", "seq"), scatter_dimension=1, tiled=True),
        lax.psum_scatter(g_out, ("batch", "seq"), scatter_dimension=1, tiled=True),
        lax.psum_scatter(g_norm_mlp, ("batch", "seq"), scatter_dimension=0, tiled=True),
        lax.psum_scatter(g_gate, ("batch", "seq"), scatter_dimension=0, tiled=True),
        lax.psum_scatter(g_up, ("batch", "seq"), scatter_dimension=0, tiled=True),
        lax.psum_scatter(g_down, ("batch", "seq"), scatter_dimension=1, tiled=True),
    )
    return (
        output[None],
        d_hidden[None],
        s_norm_attn,
        s_query,
        s_key,
        s_value,
        s_bias_q,
        s_bias_k,
        s_bias_v,
        s_out,
        s_norm_mlp,
        s_gate,
        s_up,
        s_down,
    )


def solution(mesh):
    return jax.shard_map(
        on_device,
        mesh=mesh,
        in_specs=(
            P("batch", "seq", None),
            P("batch", None),
            P(("batch", "seq")),
            P(("batch", "seq"), "tensor"),
            P(("batch", "seq"), "tensor"),
            P(("batch", "seq"), "tensor"),
            P("tensor", ("batch", "seq")),
            P("tensor", ("batch", "seq")),
            P("tensor", ("batch", "seq")),
            P("tensor", ("batch", "seq")),
            P(("batch", "seq")),
            P(("batch", "seq"), "tensor"),
            P(("batch", "seq"), "tensor"),
            P("tensor", ("batch", "seq")),
            P("batch", "seq", None),
        ),
        out_specs=(
            P("batch", "seq", None),
            P("batch", "seq", None),
            P(("batch", "seq")),
            P(("batch", "seq"), "tensor"),
            P(("batch", "seq"), "tensor"),
            P(("batch", "seq"), "tensor"),
            P("tensor", ("batch", "seq")),
            P("tensor", ("batch", "seq")),
            P("tensor", ("batch", "seq")),
            P("tensor", ("batch", "seq")),
            P(("batch", "seq")),
            P(("batch", "seq"), "tensor"),
            P(("batch", "seq"), "tensor"),
            P("tensor", ("batch", "seq")),
        ),
        check_vma=False,
    )
```

profile of v0, /device:TPU:8, one launch (start us, length us, event | category | flops | bytes accessed | tf_op | source)
XLA Modules:
  0.0 2175.3 jit_solution(14204899206872996138)
XLA Ops:
  8.8 33.4 %all_gather.45 = bf16[1536,128]{1,0:T(8,128)(2,1)S(1)} all-gather(bf16[96,128]{1,0:T(8,128)(2,1)} %param.27), channel_id=1, replica_groups=mesh['batch'=2,'seq'=8,'tensor'=2] {'batch','seq'}, dimensions={0}, use_global_device_ids=true | all-gather | bytes 417792 | tf_op jit(solution)/shard_map/all_gather | solution.py:245
  48.3 30.6 %all-reduce.10 = (bf16[128]{0:T(256)(128)(2,1)S(1)}, bf16[1536]{0:T(1024)(128)(2,1)S(1)}, bf16[128]{0:T(256)(128)(2,1)S(1)}, bf16[1536]{0:T(1024)(128)(2,1)S(1)}) all-reduce(bf16[128]{0:T(256)(128)(2,1)S(1)} %dynamic-update-slice.1, ...), channel_id=1, replica_groups=mesh['batch'=2,'seq'=8,'tensor'=2] {'batch','seq'}, use_global_device_ids=true, to_apply=%add.1 | all-reduce | flops 3328 | bytes 13312
  85.7 34.7 %all_gather.50 = bf16[1536,128]{1,0:T(8,128)(2,1)S(1)} all-gather(bf16[96,128]{1,0:T(8,128)(2,1)S(1)} %copy-done.34), channel_id=1, replica_groups=mesh['batch'=2,'seq'=8,'tensor'=2] {'batch','seq'}, dimensions={0}, use_global_device_ids=true | all-gather | bytes 417792 | tf_op jit(solution)/shard_map/all_gather | solution.py:246
  123.5 28.3 %all_gather.49 = bf16[6,128]{0,1:T(8,128)(2,1)S(1)} all-gather(bf16[6,8]{0,1:T(8,128)(2,1)S(1)} %copy.81), channel_id=1, replica_groups=mesh['batch'=2,'seq'=8,'tensor'=2] {'batch','seq'}, dimensions={1}, use_global_device_ids=true | all-gather | bytes 1632 | tf_op jit(solution)/shard_map/all_gather | solution.py:247
  154.9 15.8 all-gather.9.cloned.1.call-done
  180.9 31.1 %all-gather.11.cloned.1.call-done = bf16[4096,128]{1,0:T(8,128)(2,1)} async-done(((bf16[512,128]{1,0:T(8,128)(2,1)}), bf16[4096,128]{1,0:T(8,128)(2,1)}) %all-gather.11.cloned.1.call-update) | async-done | bytes 1048592 | tf_op jit(solution)/shard_map/all_gather | solution.py:290
  213.2 67.1 %while.39 = (s32[]{:T(128)}, f32[6,512]{1,0:T(8,128)S(1)}, f32[6,512]{1,0:T(8,128)S(1)}, f32[6,512,128]{2,1,0:T(8,128)}, s32[512]{0:T(512)S(1)}, /*index=5*/s32[...) while((s32[]{:T(128)}, f32[6,512]{1,0:T(8,128)S(1)}, ...), condition=%wide.region_12.13_spmd.clone, body=%wide.region_5.12_spmd.clone.sunk | while | flops 1654484992 | bytes 57109880 | solution.py:136
  216.6 13.4 conditional.6
  223.7 5.1 multiply_add_fusion
  233.4 13.4 conditional.6
  250.1 13.4 conditional.6
  266.9 13.4 conditional.6
  274.0 5.1 multiply_add_fusion
  292.1 47.3 %all-reduce.16.cloned.1.call-done = bf16[512,1536]{1,0:T(8,128)(2,1)} async-done(((bf16[512,1536]{1,0:T(8,128)(2,1)}), bf16[512,1536]{1,0:T(8,128)(2,1)}) %all-reduce.16.cloned.1.call-update) | async-done | bytes 1572880 | tf_op jit(solution)/shard_map/psum | solution.py:299
  343.3 105.1 %all-gather.15.cloned.1.call-done = bf16[1536,4480]{1,0:T(8,128)(2,1)} async-done(((bf16[96,4480]{1,0:T(8,128)(2,1)}), bf16[1536,4480]{1,0:T(8,128)(2,1)}) %all-gather.15.cloned.1.call-update) | async-done | bytes 13762576 | tf_op jit(solution)/shard_map/all_gather | solution.py:252
  448.4 13.2 fusion.165
  461.6 95.7 %all-gather.17.cloned.1.call-done = bf16[1536,4480]{1,0:T(8,128)(2,1)} async-done(((bf16[96,4480]{1,0:T(8,128)(2,1)}), bf16[1536,4480]{1,0:T(8,128)(2,1)}) %all-gather.17.cloned.1.call-update) | async-done | bytes 13762576 | tf_op jit(solution)/shard_map/all_gather | solution.py:253
  557.2 13.2 fusion.166
  570.4 95.7 %all-gather.19.cloned.1.call-done = bf16[4480,1536]{0,1:T(8,128)(2,1)} async-done(((bf16[4480,96]{0,1:T(8,128)(2,1)}), bf16[4480,1536]{0,1:T(8,128)(2,1)}) %all-gather.19.cloned.1.call-update) | async-done | bytes 13762576 | tf_op jit(solution)/shard_map/all_gather | solution.py:254
  666.1 21.8 %multiply_convert_fusion = (bf16[512,4480]{1,0:T(8,128)(2,1)}, bf16[512,4480]{1,0:T(8,128)(2,1)}, bf16[512,4480]{1,0:T(8,128)(2,1)}) fusion(f32[512,4480]{1,0:T(8,128)} %fusion.165, f32[512,4480]{1,0:T(8,128)} %fusion.166, bf16[4480,1536]{0,1:T(8,128)(2,1)} %all-gather.19.cloned.1.call-done, bf16[1,512,1536]{2,1,0:T(8,128)(2,1)} %param.37), kind=kOutput, calls=%fused_computation.144 | convolution fusion | flops 7080837120 | bytes 47448064 | tf_op jit(solution)/shard_map/dot_general | solution.py:317
  687.9 11.8 fusion.167
  699.7 11.7 fusion.109
  712.1 50.6 %all-reduce.18.cloned.1.call-done = bf16[512,1536]{1,0:T(8,128)(2,1)} async-done(((bf16[512,1536]{1,0:T(8,128)(2,1)}), bf16[512,1536]{1,0:T(8,128)(2,1)}) %all-reduce.18.cloned.1.call-update) | async-done | bytes 1572880 | tf_op jit(solution)/shard_map/psum | solution.py:325
  773.6 98.7 %while.40 = (s32[]{:T(128)}, f32[512,6,128]{2,0,1:T(8,128)S(1)}, bf16[4,1024,128]{2,1,0:T(8,128)(2,1)}, bf16[4,1024,128]{2,1,0:T(8,128)(2,1)}, s32[512]{0:T(512)...) while((s32[]{:T(128)}, f32[512,6,128]{2,0,1:T(8,128)S(1)}, ...), condition=%wide.region_23.24_spmd.clone, body=%wide.region_18.23_spmd.clone.sunk | while | flops 4061222912 | bytes 86888936 | solution.py:199
  778.3 19.1 conditional.7
  782.0 5.4 fusion.23
  803.0 19.1 conditional.7
  806.6 5.4 fusion.23
  827.6 19.1 conditional.7
  831.3 5.4 fusion.23
  852.3 19.1 conditional.7
  856.0 5.4 fusion.23
  875.4 13.2 convolution_convert_fusion
  894.3 41.4 %reduce-scatter.13.cloned.1.call-done = bf16[512,128]{0,1:T(8,128)(2,1)} async-done(((bf16[4096,128]{0,1:T(8,128)(2,1)}), bf16[512,128]{0,1:T(8,128)(2,1)}) %reduce-scatter.13.cloned.1.call-update) | async-done | bytes 131088 | tf_op jit(solution)/shard_map/reduce_scatter | solution.py:361
  941.5 60.4 %reduce-scatter.15.cloned.1.call-done = bf16[512,128]{1,0:T(8,128)(2,1)} async-done(((bf16[4096,128]{1,0:T(8,128)(2,1)}), bf16[512,128]{1,0:T(8,128)(2,1)}) %reduce-scatter.15.cloned.1.call-update) | async-done | bytes 131088 | tf_op jit(solution)/shard_map/reduce_scatter | solution.py:364
  1014.3 6.5 fusion.119
  1020.8 16.1 fusion.169
  1037.0 15.5 fusion.170
  1052.6 16.2 fusion.113
  1070.3 20.6 all-reduce.20.cloned.1.call-done
  1093.5 59.4 %all-reduce.9 = (f32[1536]{0:T(1024)S(1)}, f32[6,128]{1,0:T(8,128)S(1)}, f32[1,128]{1,0:T(1,128)S(1)}, f32[1,128]{1,0:T(1,128)S(1)}, f32[1536]{0:T(1024)S(1)}) all-reduce(f32[1536]{0:T(1024)S(1)} %get-tuple-element.803, f32[6,128]{1,0:T(8,128)S(1)} %get-tuple-element.874, ...), channel_id=5, replica_groups=mesh['batch'=2,'seq'=8,'tensor'=2] {'batch','seq'}, use_global_device_ids=true, to_apply=%region_29.30.clone | all-reduce | flops 4096 | bytes 32768
  1155.3 5.8 fusion.93
  1161.2 50.4 %reduce-scatter.21.cloned.1.call-done = f32[96,128]{1,0:T(8,128)} async-done(((f32[1536,128]{1,0:T(8,128)}), f32[96,128]{1,0:T(8,128)}) %reduce-scatter.21.cloned.1.call-update) | async-done | bytes 49168 | tf_op jit(solution)/shard_map/reduce_scatter | solution.py:412
  1211.5 78.9 %reduce-scatter.17.cloned.1.call-done = f32[96,768]{1,0:T(8,128)} async-done(((f32[1536,768]{1,0:T(8,128)}), f32[96,768]{1,0:T(8,128)}) %reduce-scatter.17.cloned.1.call-update) | async-done | bytes 294928 | tf_op jit(solution)/shard_map/reduce_scatter | solution.py:410
  1290.4 78.9 %reduce-scatter.23.cloned.1.call-done = f32[768,96]{0,1:T(8,128)} async-done(((f32[768,1536]{0,1:T(8,128)}), f32[768,96]{0,1:T(8,128)}) %reduce-scatter.23.cloned.1.call-update) | async-done | bytes 294928 | tf_op jit(solution)/shard_map/reduce_scatter | solution.py:416
  1369.3 265.7 %reduce-scatter.25.cloned.1.call-done = f32[96,4480]{1,0:T(8,128)} async-done(((f32[1536,4480]{1,0:T(8,128)}), f32[96,4480]{1,0:T(8,128)}) %reduce-scatter.25.cloned.1.call-update) | async-done | bytes 1720336 | tf_op jit(solution)/shard_map/reduce_scatter | solution.py:418
  1635.0 266.5 %reduce-scatter.27.cloned.1.call-done = f32[96,4480]{1,0:T(8,128)} async-done(((f32[1536,4480]{1,0:T(8,128)}), f32[96,4480]{1,0:T(8,128)}) %reduce-scatter.27.cloned.1.call-update) | async-done | bytes 1720336 | tf_op jit(solution)/shard_map/reduce_scatter | solution.py:419
  1901.5 267.1 %reduce-scatter.29.cloned.1.call-done = f32[4480,96]{0,1:T(8,128)} async-done(((f32[4480,1536]{0,1:T(8,128)}), f32[4480,96]{0,1:T(8,128)}) %reduce-scatter.29.cloned.1.call-update) | async-done | bytes 1720336 | tf_op jit(solution)/shard_map/reduce_scatter | solution.py:420
  (344 shorter events, 212.2 us)
Async XLA Ops:
  7.2 78.5 %copy-start.34 = (bf16[96,128]{1,0:T(8,128)(2,1)S(1)}, bf16[96,128]{1,0:T(8,128)(2,1)}, u32[]{:S(2)}) copy-start(bf16[96,128]{1,0:T(8,128)(2,1)} %param.28) | copy-start | bytes 73732
  7.2 145.2 %all-gather.21.cloned.1.call-start = ((), (), s32[]{:S(2)}) async-start(), calls=%async_computation.26 | async-start | bytes 1179648 | tf_op jit(solution)/shard_map/all_gather | solution.py:289
  7.3 144.6 %copy-start.41 = (f32[64]{0:T(128)}, f32[64]{0:T(128)S(1)}, u32[]{:S(2)}) copy-start(f32[64]{0:T(128)S(1)} %multiply_power_fusion) | copy-start | bytes 772
  42.2 80.4 %copy-start.14 = (bf16[1536,128]{1,0:T(8,128)(2,1)}, bf16[1536,128]{1,0:T(8,128)(2,1)S(1)}, u32[]{:S(2)}) copy-start(bf16[1536,128]{1,0:T(8,128)(2,1)S(1)} %all_gather.45) | copy-start | bytes 1179652
  42.2 79.1 %copy-start.2 = (bf16[1,512,1536]{2,1,0:T(8,128)(2,1)S(1)}, bf16[1,512,1536]{2,1,0:T(8,128)(2,1)}, u32[]{:S(2)}) copy-start(bf16[1,512,1536]{2,1,0:T(8,128)(2,1)} %param.23) | copy-start | bytes 4718596
  78.9 91.8 %copy-start.23 = (f32[1536]{0:T(1024)}, f32[1536]{0:T(1024)S(1)}, u32[]{:S(2)}) copy-start(f32[1536]{0:T(1024)S(1)} %convert_element_type.190) | copy-start | bytes 18436
  81.3 89.4 %copy-start.27 = (f32[512]{0:T(512)}, f32[512]{0:T(512)S(1)}, u32[]{:S(2)}) copy-start(f32[512]{0:T(512)S(1)} %get-tuple-element.896) | copy-start | bytes 6148
  81.5 70.4 %copy-start.31 = (f32[512]{0:T(512)}, f32[512]{0:T(512)S(1)}, u32[]{:S(2)}) copy-start(f32[512]{0:T(512)S(1)} %subtract_convert_fusion.1) | copy-start | bytes 6148
  83.6 39.5 %copy-start.46 = (s32[1,7]{1,0:T(1,128)S(1)}, s32[1,7]{1,0:T(1,128)}, u32[]{:S(2)}) copy-start(s32[1,7]{1,0:T(1,128)} %param.24) | copy-start | bytes 88
  83.6 39.7 %copy-start.43 = (bf16[6,8]{1,0:T(8,128)(2,1)S(1)}, bf16[6,8]{1,0:T(8,128)(2,1)}, u32[]{:S(2)}) copy-start(bf16[6,8]{1,0:T(8,128)(2,1)} %param.29) | copy-start | bytes 292
  84.9 85.8 %all-gather.9.cloned.1.call-start = ((), (), s32[]{:S(2)}) async-start(), calls=%async_computation.9 | async-start | bytes 2506752 | tf_op jit(solution)/shard_map/all_gather | solution.py:244
  85.7 126.3 %all-gather.11.cloned.1.call-start = ((), (), s32[]{:S(2)}) async-start(), calls=%async_computation.10 | async-start | bytes 1179648 | tf_op jit(solution)/shard_map/all_gather | solution.py:290
  122.5 162.4 %all-gather.13.cloned.1.call-start = ((), (), s32[]{:S(2)}) async-start(), calls=%async_computation.11 | async-start | bytes 2506752 | tf_op jit(solution)/shard_map/all_gather | solution.py:250
  123.1 216.2 %all-reduce.16.cloned.1.call-start = ((), (), s32[]{:S(2)}) async-start(), calls=%async_computation.12 | async-start | bytes 3145728 | tf_op jit(solution)/shard_map/psum | solution.py:299
  152.4 25.6 %copy-start.16 = (f32[512,64]{0,1:T(8,128)}, f32[512,64]{0,1:T(8,128)S(1)}, u32[]{:S(2)}) copy-start(f32[512,64]{0,1:T(8,128)S(1)} %get-tuple-element.893) | copy-start | bytes 393220
  152.4 25.6 %copy-start.18 = (f32[512,64]{0,1:T(8,128)}, f32[512,64]{0,1:T(8,128)S(1)}, u32[]{:S(2)}) copy-start(f32[512,64]{0,1:T(8,128)S(1)} %get-tuple-element.894) | copy-start | bytes 393220
  284.9 4.6 copy-start.21
  289.5 158.9 %all-gather.15.cloned.1.call-start = ((), (), s32[]{:S(2)}) async-start(), calls=%async_computation.13 | async-start | bytes 14622720 | tf_op jit(solution)/shard_map/all_gather | solution.py:252
  290.1 267.1 %all-gather.17.cloned.1.call-start = ((), (), s32[]{:S(2)}) async-start(), calls=%async_computation.14 | async-start | bytes 14622720 | tf_op jit(solution)/shard_map/all_gather | solution.py:253
  290.8 375.2 %all-gather.19.cloned.1.call-start = ((), (), s32[]{:S(2)}) async-start(), calls=%async_computation.15 | async-start | bytes 14622720 | tf_op jit(solution)/shard_map/all_gather | solution.py:254
  291.6 471.2 %all-reduce.18.cloned.1.call-start = ((), (), s32[]{:S(2)}) async-start(), calls=%async_computation.16 | async-start | bytes 3145728 | tf_op jit(solution)/shard_map/psum | solution.py:325
  292.0 474.5 %copy-start.25 = (f32[1536]{0:T(1024)}, f32[1536]{0:T(1024)S(1)}, u32[]{:S(2)}) copy-start(f32[1536]{0:T(1024)S(1)} %convert_element_type.201) | copy-start | bytes 18436
  341.5 425.1 %copy-start.29 = (f32[512]{0:T(512)}, f32[512]{0:T(512)S(1)}, u32[]{:S(2)}) copy-start(f32[512]{0:T(512)S(1)} %get-tuple-element.898) | copy-start | bytes 6148
  341.5 425.1 %copy-start.37 = (f32[512]{0:T(512)}, f32[512]{0:T(512)S(1)}, u32[]{:S(2)}) copy-start(f32[512]{0:T(512)S(1)} %get-tuple-element.897) | copy-start | bytes 6148
  687.9 11.8 copy-start.47
  711.5 224.3 %reduce-scatter.13.cloned.1.call-start = ((), (), s32[]{:S(2)}) async-start(), calls=%async_computation.17 | async-start | bytes 1179648 | tf_op jit(solution)/shard_map/reduce_scatter | solution.py:361
  762.8 4.4 copy-start.11
  762.8 4.4 copy-start.45
  803.0 3.6 copy-start
  827.7 3.6 copy-start
  874.6 127.3 %reduce-scatter.15.cloned.1.call-start = ((), (), s32[]{:S(2)}) async-start(), calls=%async_computation.18 | async-start | bytes 1179648 | tf_op jit(solution)/shard_map/reduce_scatter | solution.py:364
  875.3 215.6 %all-reduce.20.cloned.1.call-start = ((), (), s32[]{:S(2)}) async-start(), calls=%async_computation.27 | async-start | bytes 6291456 | tf_op jit(solution)/shard_map/psum | solution.py:311
  891.2 45.4 %copy-start.32 = (f32[512]{0:T(512)S(1)}, f32[512]{0:T(512)}, u32[]{:S(2)}) copy-start(f32[512]{0:T(512)} %copy-done.31) | copy-start | bytes 6148
  891.2 45.4 %copy-start.42 = (f32[64]{0:T(128)S(1)}, f32[64]{0:T(128)}, u32[]{:S(2)}) copy-start(f32[64]{0:T(128)} %copy-done.41) | copy-start | bytes 772
  891.2 46.0 %copy-start.15 = (bf16[1536,128]{1,0:T(8,128)(2,1)S(1)}, bf16[1536,128]{1,0:T(8,128)(2,1)}, u32[]{:S(2)}) copy-start(bf16[1536,128]{1,0:T(8,128)(2,1)} %copy-done.14) | copy-start | bytes 1179652
  937.2 64.7 %copy-start.13 = (bf16[1536,128]{1,0:T(8,128)(2,1)S(1)}, bf16[1536,128]{1,0:T(8,128)(2,1)}, u32[]{:S(2)}) copy-start(bf16[1536,128]{1,0:T(8,128)(2,1)} %copy-done.12) | copy-start | bytes 1179652
  941.5 64.2 %copy-start.3 = (bf16[1,512,1536]{2,1,0:T(8,128)(2,1)S(1)}, bf16[1,512,1536]{2,1,0:T(8,128)(2,1)}, u32[]{:S(2)}) copy-start(bf16[1,512,1536]{2,1,0:T(8,128)(2,1)} %param.23) | copy-start | bytes 4718596
  941.5 64.2 %copy-start.24 = (f32[1536]{0:T(1024)S(1)}, f32[1536]{0:T(1024)}, u32[]{:S(2)}) copy-start(f32[1536]{0:T(1024)} %copy-done.23) | copy-start | bytes 18436
  941.5 64.2 %copy-start.28 = (f32[512]{0:T(512)S(1)}, f32[512]{0:T(512)}, u32[]{:S(2)}) copy-start(f32[512]{0:T(512)} %copy-done.27) | copy-start | bytes 6148
  1005.6 155.5 %reduce-scatter.19.cloned.1.call-start = ((), (), s32[]{:S(2)}) async-start(), calls=%async_computation.20 | async-start | bytes 835584 | tf_op jit(solution)/shard_map/reduce_scatter | solution.py:411
  1007.3 204.2 %reduce-scatter.21.cloned.1.call-start = ((), (), s32[]{:S(2)}) async-start(), calls=%async_computation.21 | async-start | bytes 835584 | tf_op jit(solution)/shard_map/reduce_scatter | solution.py:412
  1009.1 281.3 %reduce-scatter.17.cloned.1.call-start = ((), (), s32[]{:S(2)}) async-start(), calls=%async_computation.19 | async-start | bytes 5013504 | tf_op jit(solution)/shard_map/reduce_scatter | solution.py:410
  1012.9 356.4 %reduce-scatter.23.cloned.1.call-start = ((), (), s32[]{:S(2)}) async-start(), calls=%async_computation.22 | async-start | bytes 5013504 | tf_op jit(solution)/shard_map/reduce_scatter | solution.py:416
  1020.8 614.2 %reduce-scatter.25.cloned.1.call-start = ((), (), s32[]{:S(2)}) async-start(), calls=%async_computation.23 | async-start | bytes 29245440 | tf_op jit(solution)/shard_map/reduce_scatter | solution.py:418
  1036.9 864.6 %reduce-scatter.27.cloned.1.call-start = ((), (), s32[]{:S(2)}) async-start(), calls=%async_computation.24 | async-start | bytes 29245440 | tf_op jit(solution)/shard_map/reduce_scatter | solution.py:419
  1052.5 1116.1 %reduce-scatter.29.cloned.1.call-start = ((), (), s32[]{:S(2)}) async-start(), calls=%async_computation.25 | async-start | bytes 29245440 | tf_op jit(solution)/shard_map/reduce_scatter | solution.py:420
  1068.8 24.7 %copy-start.33 = (f32[1536]{0:T(1024)S(1)}, f32[1536]{0:T(1024)}, u32[]{:S(2)}) copy-start(f32[1536]{0:T(1024)} %get-tuple-element.801) | copy-start | bytes 18436
  1068.8 86.5 %copy-start.36 = (f32[512]{0:T(512)S(1)}, f32[512]{0:T(512)}, u32[]{:S(2)}) copy-start(f32[512]{0:T(512)} %get-tuple-element.895) | copy-start | bytes 6148
  (43 other events, 102.9 us)
Sparse Core Ops, SparseCore 0:
  85.0 42.0 all-gather.20
  129.3 41.3 all-gather.8
  173.4 38.5 all-gather.10
  214.0 41.4 all-gather.12
  289.6 49.6 all-reduce.15
  341.7 106.6 all-gather.14
  450.8 106.3 all-gather.16
  559.7 106.3 all-gather.18
  711.6 51.1 all-reduce.17
  874.7 60.9 reduce-scatter.12
  939.5 62.3 reduce-scatter.14
  1005.7 85.1 all-reduce.19
  1095.4 56.5 reduce-scatter.18
  1156.0 55.5 reduce-scatter.20
  1216.3 74.0 reduce-scatter.16
  1294.7 74.5 reduce-scatter.22
  1374.4 260.5 reduce-scatter.24
  1639.5 261.9 reduce-scatter.26
  1906.7 261.8 reduce-scatter.28
where the time goes:
time: 2190 us; the launch traced here: 2180 us
  waiting for transfers between devices  1580 us (72%)
  matrix products  285 us (13%)
  blocking collectives  186 us (8%)
  other arithmetic  55.5 us (3%)
  local copies, waits for them, and re-layouts  43 us (2%)
    reduce_scatter x1, waiting for transfers between devices, on_device(): lax.psum_scatter(g_down, ('batch', 'seq'), scatter_dimension=1, tiled=True)  267 us
    reduce_scatter x1, waiting for transfers between devices, on_device(): lax.psum_scatter(g_up, ('batch', 'seq'), scatter_dimension=0, tiled=True)  266 us
    reduce_scatter x1, waiting for transfers between devices, on_device(): lax.psum_scatter(g_gate, ('batch', 'seq'), scatter_dimension=0, tiled=True)  266 us
    all_gather x1, waiting for transfers between devices, on_device(): lax.all_gather(w_gate, ('batch', 'seq'), axis=0, tiled=True)  105 us
    all_gather x1, waiting for transfers between devices, on_device(): lax.all_gather(w_down, ('batch', 'seq'), axis=1, tiled=True)  95.7 us
    all_gather x1, waiting for transfers between devices, on_device(): lax.all_gather(w_up, ('batch', 'seq'), axis=0, tiled=True)  95.7 us
    unnamed x2, blocking collectives  90 us
    reduce_scatter x1, waiting for transfers between devices, on_device(): lax.psum_scatter(g_out, ('batch', 'seq'), scatter_dimension=1, tiled=True)  78.9 us
  transfers between devices with their start and end apart: 19, of which 16 were waited for; matrix products, arithmetic and copies ran while one was open for 9% of the time, Pallas kernels for 0%

commit v1 on v0

v1 whole, which is shorter than its diff:
```python
import functools

import jax
import jax.numpy as jnp
from jax import lax
from jax.experimental import pallas as pl
from jax.experimental.pallas import tpu as pltpu
from jax.sharding import Mesh
from jax.sharding import PartitionSpec as P

HEAD_SIZE = 128
NORM_EPS = 1e-06
ROPE_BASE = 10000.0
MASKED = -1e30
FLOOR = -1e29
FC = 256
BF = jnp.bfloat16
F32 = jnp.float32
VMEM = pl.BlockSpec(memory_space=pltpu.VMEM)


def row_positions(stored, shards, half_rows):
    slot_id = stored // half_rows
    inner = stored % half_rows
    shard_id = slot_id // 2
    row_block = jnp.where(slot_id % 2 == 0, shard_id, 2 * shards - 1 - shard_id)
    return row_block * half_rows + inner


def doc_starts_of(row_pos, doc_lengths):
    doc_ends = jnp.cumsum(doc_lengths)
    doc_starts = doc_ends - doc_lengths
    inside = (row_pos[:, None] >= doc_starts[None, :]) & (row_pos[:, None] < doc_ends[None, :])
    return jnp.sum(jnp.where(inside, doc_starts[None, :], 0), axis=1).astype(jnp.int32)


def rotary(doc_pos, head_dim):
    half_dim = head_dim // 2
    freqs = ROPE_BASE ** (-2.0 * jnp.arange(half_dim, dtype=jnp.float32) / head_dim)
    angles = doc_pos.astype(jnp.float32)[:, None] * freqs[None, :]
    return (jnp.cos(angles), jnp.sin(angles))


def norm_factor(resid):
    return lax.rsqrt(jnp.mean(resid * resid, axis=-1, keepdims=True) + NORM_EPS)


def norm_backward(resid, factor, gain, grad_in):
    weighted = grad_in * gain
    grad_resid = factor * weighted - resid * factor**3 * jnp.mean(
        weighted * resid, axis=-1, keepdims=True
    )
    grad_gain = jnp.sum(grad_in * resid * factor, axis=0, keepdims=True)
    return (grad_resid, grad_gain)


def dot(a, b):
    return jnp.dot(a, b, preferred_element_type=F32)


def dot_nt(a, b):
    return lax.dot_general(a, b, (((1,), (1,)), ((), ())), preferred_element_type=F32)


def block_mask(sub, block, me, shards, half, start_row, heads):
    key_blk = jnp.where(sub == 0, block, 2 * shards - 1 - block)
    query_blk = jnp.where(sub == 0, me, 2 * shards - 1 - me)
    key_pos = key_blk * half + lax.broadcasted_iota(jnp.int32, (half, half), 0)
    query_pos = query_blk * half + lax.broadcasted_iota(jnp.int32, (half, half), 1)
    allowed = (key_pos <= query_pos) & (key_pos >= start_row)
    return jnp.concatenate([jnp.where(allowed, 0.0, MASKED).astype(F32)] * heads, axis=1)


def stack_heads(ref, sub, half, heads):
    return jnp.concatenate(
        [
            ref[sub * half : (sub + 1) * half, h * HEAD_SIZE : (h + 1) * HEAD_SIZE]
            for h in range(heads)
        ],
        axis=0,
    )


class Pool:
    def __init__(self, ref):
        self.ref, self.used = ref, 0

    def take(self, count=1):
        base = self.used
        self.used += count
        assert self.used <= self.ref.shape[0], self.used
        return lambda i=0: self.ref.at[base + i]


def merge_rows(value):
    homes, rows, cols = value.shape
    if rows % 16:
        return value.astype(F32).reshape(homes * rows, cols).astype(BF)
    return value.reshape(homes * rows, cols)


class Spread:
    def __init__(self, zs, src, buf, pool):
        self.zs, self.src, self.buf = zs, src, buf
        self.b, self.z, self.x = (lax.axis_index(a) for a in ("batch", "z", "x"))
        self.up_s, self.dn_s, self.z_r, self.x_s, self.x_r = (pool.take(zs) for _ in range(5))
        self.s_s, self.s_r = pool.take(2 * zs), pool.take(2 * zs)
        self.loc = pool.take()

    def at(self, b, z, x):
        return self.buf.at[(b * self.zs + z) * 2 + x]

    def up(self, s, src=None):
        dst = self.at(self.b, s, self.x)
        src = dst if src is None else src
        return remote(src, dst, self.up_s(s), self.z_r(s), {"z": self.z + 1})

    def dn(self, s, src=None):
        dst = self.at(self.b, s, self.x)
        src = dst if src is None else src
        return remote(src, dst, self.dn_s(s), self.z_r(s), {"z": self.z - 1})

    def side(self, s, src=None):
        dst = self.at(self.b, s, self.x)
        src = dst if src is None else src
        return remote(src, dst, self.x_s(s), self.x_r(s), {"x": 1 - self.x})

    def sib(self, s, far=0, src=None):
        dst = self.at(self.b, s, self.x if far == 0 else 1 - self.x)
        src = dst if src is None else src
        i = far * self.zs + s
        return remote(src, dst, self.s_s(i), self.s_r(i), {"batch": 1 - self.b})

    def local(self):
        return pltpu.make_async_copy(self.src, self.at(self.b, self.z, self.x), self.loc())

    def start(self):
        @pl.when(self.z < self.zs - 1)
        def _():
            self.up(self.z, self.src).start()

        @pl.when(self.z > 0)
        def _():
            self.dn(self.z, self.src).start()

        self.side(self.z, self.src).start()
        self.sib(self.z, 0, self.src).start()
        self.local().start()

    def hop(self, k):
        low, high = self.z - k, self.z + k

        @pl.when(low >= 0)
        def _():
            self.dn(low).wait_recv()

            @pl.when(self.z < self.zs - 1)
            def _():
                self.up(low).start()

            self.side(low).start()
            self.sib(low).start()

        @pl.when(high < self.zs)
        def _():
            self.dn(high).wait_recv()

            @pl.when(self.z > 0)
            def _():
                self.dn(high).start()

            self.side(high).start()
            self.sib(high).start()

    def cross(self):
        for s in range(self.zs):
            dst = self.at(self.b, s, 1 - self.x)
            remote(dst, dst, self.x_s(s), self.x_r(s), {"x": 1 - self.x}).wait_recv()
            self.sib(s, 1).start()

    def finish(self):
        self.local().wait()
        for far in range(2):
            for s in range(self.zs):
                dst = self.at(1 - self.b, s, self.x if far == 0 else 1 - self.x)
                i = far * self.zs + s
                remote(dst, dst, self.s_s(i), self.s_r(i), {"batch": 1 - self.b}).wait_recv()

    def drain(self):
        for s in range(self.zs):

            @pl.when((s <= self.z) & (self.z < self.zs - 1))
            def _():
                self.up(s).wait_send()

            @pl.when((s >= self.z) & (self.z > 0))
            def _():
                self.dn(s).wait_send()

            self.side(s).wait_send()
            self.sib(s, 0).wait_send()
            self.sib(s, 1).wait_send()


def lanes(vec, first, count):
    return jnp.concatenate([vec[r : r + 1, :] for r in range(first, first + count)], axis=1)


def thirds(zs):
    hops = list(range(1, zs))
    per = -(-len(hops) // 3)
    return [hops[i * per : (i + 1) * per] for i in range(3)]


def forward_kernel(
    zs,
    heads,
    n1,
    skip,
    scale,
    x_ref,
    wqkv_in,
    wo_in,
    small_in,
    cos_ref,
    sin_ref,
    start_ref,
    dy_in,
    *refs,
):
    refs = list(refs)
    if n1:
        mats = refs[:3]
        del refs[:3]
    h1_out, q_out, attn_out, lse_out, mid_out, vec_out = refs[:6]
    wqkv_all, wo_all, kv_all, h2_all, dy_all = refs[6:11]
    del refs[:11]
    if n1:
        full = refs.pop(0)
    small_buf, wqkv_buf, wo_buf, kv_buf, q_t, acc_ref, max_ref, sum_ref = refs[:8]
    att_send, att_recv, h2_half, xn_ref, sem_ref = refs[8:13]
    g_sems = refs[13:]
    b, z, x, t = (lax.axis_index(a) for a in ("batch", "z", "x", "tensor"))
    shards = 2 * zs
    me = 2 * z + x
    tok, width = x_ref.shape
    half = tok // 2
    q_cols = heads * HEAD_SIZE
    pool = Pool(sem_ref)
    greet(z, zs)

    small = Spread(zs, small_in, small_buf, pool)
    wqkv = Spread(zs, wqkv_in, wqkv_buf, pool)
    wo = Spread(zs, wo_in, wo_buf, pool)
    small.start()
    wqkv.start()
    wo.start()

    runs = thirds(zs)
    if n1:
        trade = Exchange(mats, full, 0, zs, skip, [pool.take(n1) for _ in range(3)])
        gather = Gather(zs, None, full, [None] + list(g_sems))
        for c in range(n1):
            trade.keep(c, c)

    def ship(first, last):
        if n1:
            for c in range(first, last):
                trade.ship(c, c)

    def prefetch(tick):
        if n1:
            for c in range(n1):
                hops = [k for k in range(1, zs) if min(k, 3) == tick - c]
                if tick == c:
                    trade.arrived(c, c)
                    gather.start(c)
                for k in hops:
                    gather.hop(c, k)

    quarter = half // 2
    dy_l, dyy_s, dyy_r = (pool.take() for _ in range(3))
    dyx_s, dyx_r = pool.take(3), pool.take(3)
    dy_own = pltpu.make_async_copy(dy_in, dy_all.at[pl.ds(2 * x, 2)], dy_l())
    dy_own.start()

    def dy_side(i):
        rows = pl.ds((i % 3 > 0) * quarter, quarter)
        block = t if i < 2 else 1 - t
        dst = dy_all.at[2 * x + block, rows]
        return remote(dy_in.at[block, rows], dst, dyx_s(i), dyx_r(i), {"x": 1 - x})

    dy_piece = dy_all.at[2 * (1 - x) + t, pl.ds(0, quarter)]
    dy_across = remote(dy_piece, dy_piece, dyy_s(), dyy_r(), {"tensor": 1 - t})

    ship(0, 2)
    for m in range(2):
        at = slice(m * half, (m + 1) * half)
        xv = x_ref[at].astype(F32)
        xn_ref[at] = xv * norm_factor(xv)
    for k in range(1, zs):
        small.hop(k)
        wqkv.hop(k)
    prefetch(0)
    ship(2, 3)
    for k in runs[0]:
        wo.hop(k)
    small.cross()
    small.finish()
    vec = jnp.sum(small_buf[...].astype(F32), axis=0)
    vec_out[...] = vec
    bias = lanes(vec, 0, 4)
    gain_attn = lanes(vec, 4, 6)
    gain_mlp = lanes(vec, 10, 6)
    for m in range(2):
        at = slice(m * half, (m + 1) * half)
        h1_out[at] = (xn_ref[at] * gain_attn).astype(BF)

    wqkv.cross()
    prefetch(1)
    wqkv.finish()
    wqkv_m = merge_rows(wqkv_buf[...])
    for m in range(2):
        at = slice(m * half, (m + 1) * half)
        lin = dot(h1_out[at], wqkv_m) + bias
        cos, sin = cos_ref[at], sin_ref[at]
        for h in range(heads + 1):
            v = lin[:, h * HEAD_SIZE : (h + 1) * HEAD_SIZE]
            v = (v * cos + pltpu.roll(v, HEAD_SIZE // 2, 1) * sin).astype(BF)
            if h < heads:
                q_out[at, h * HEAD_SIZE : (h + 1) * HEAD_SIZE] = v
            else:
                kv_buf[me + m, :, :HEAD_SIZE] = v
        kv_buf[me + m, :, HEAD_SIZE:] = lin[:, (heads + 1) * HEAD_SIZE :].astype(BF)

    ku_s, kd_s, k0_r, k1_r, x0_s, x1_s, x0_r, x1_r = (pool.take(zs) for _ in range(8))

    def kv_up(s):
        piece = kv_buf.at[2 * s + x]
        return remote(piece, piece, ku_s(s), k0_r(s), {"z": z + 1})

    def kv_dn(s):
        piece = kv_buf.at[2 * s + x + 1]
        return remote(piece, piece, kd_s(s), k1_r(s), {"z": z - 1})

    def kv_side(s, sub, col):
        piece = kv_buf.at[2 * s + col + sub]
        send, recv = (x0_s, x0_r) if sub == 0 else (x1_s, x1_r)
        return remote(piece, piece, send(s), recv(s), {"x": 1 - x})

    @pl.when(z < zs - 1)
    def _():
        kv_up(z).start()

    @pl.when(z > 0)
    def _():
        kv_dn(z).start()

    @pl.when(x == 0)
    def _():
        kv_side(z, 0, x).start()

    @pl.when(x == 1)
    def _():
        kv_side(z, 1, x).start()

    for k in runs[1]:
        wo.hop(k)
    for sub in range(2):
        q_t[sub] = stack_heads(q_out, sub, half, heads).T
    acc_ref[...] = jnp.zeros_like(acc_ref)
    max_ref[...] = jnp.full_like(max_ref, FLOOR)
    sum_ref[...] = jnp.zeros_like(sum_ref)

    def fold(sub, block):
        keys = kv_buf[block + sub, :, :HEAD_SIZE]
        vals = kv_buf[block + sub, :, HEAD_SIZE:]
        start_row = start_ref[:, sub * half : (sub + 1) * half]
        scores = dot(keys, q_t[sub]) * scale + block_mask(
            sub, block, me, shards, half, start_row, heads
        )
        old_max = max_ref[sub]
        new_max = jnp.maximum(old_max, jnp.max(scores, axis=0, keepdims=True))
        weights = jnp.exp(scores - new_max)
        shrink = jnp.exp(old_max - new_max)
        max_ref[sub] = new_max
        sum_ref[sub] = sum_ref[sub] * shrink + jnp.sum(weights, axis=0, keepdims=True)
        acc_ref[sub] = acc_ref[sub] * shrink + dot(vals.T, weights.astype(BF))

    def attend(k, carry):
        low, high = z - k, z + k

        @pl.when((low >= 0) & (k < zs))
        def _():
            @pl.when(k > 0)
            def _():
                kv_up(low).wait_recv()

                @pl.when(z < zs - 1)
                def _():
                    kv_up(low).start()

                kv_side(low, 0, x).start()

        @pl.when((high < zs) & (k < zs))
        def _():
            @pl.when(k > 0)
            def _():
                kv_dn(high).wait_recv()

                @pl.when(z > 0)
                def _():
                    kv_dn(high).start()

                kv_side(high, 1, x).start()

        @pl.when((low >= 0) & (k < zs))
        def _():
            fold(0, 2 * low + x)

        @pl.when((high < zs) & (k < zs))
        def _():
            fold(1, 2 * high + x)

        far_low, far_high = low + 1, high - 1

        @pl.when((k > 0) & (far_low >= 0) & ((k > 1) | (x == 1)))
        def _():
            kv_side(far_low, 0, 1 - x).wait_recv()
            fold(0, 2 * far_low + 1 - x)

        @pl.when((k > 0) & (far_high < zs) & ((k > 1) | (x == 0)))
        def _():
            kv_side(far_high, 1, 1 - x).wait_recv()
            fold(1, 2 * far_high + 1 - x)

        @pl.when(k == 1)
        def _():
            for hop in runs[2]:
                wo.hop(hop)

        @pl.when(k == 2)
        def _():
            prefetch(2)

        @pl.when(k == zs - 1)
        def _():
            ship(3, n1)

        return carry

    lax.fori_loop(0, zs + 1, attend, 0)
    wo.cross()
    for sub in range(2):
        lse_out[sub : sub + 1, :] = max_ref[sub] + jnp.log(sum_ref[sub])
        out_t = acc_ref[sub] / sum_ref[sub]
        for h in range(heads):
            attn_out[sub * half : (sub + 1) * half, h * HEAD_SIZE : (h + 1) * HEAD_SIZE] = (
                out_t[:, h * half : (h + 1) * half].T.astype(BF)
            )

    dy_side(1).start()
    dy_side(0).start()
    wo.finish()
    att_s, att_r = pool.take(2), pool.take(2)
    h_l, hx_s, hx_r, hy_s, hy_r = (pool.take(2) for _ in range(5))
    hxx_s, hxx_r, hyy_s, hyy_r = (pool.take() for _ in range(4))

    def rows(i):
        return pl.ds(i * quarter, quarter)

    def att_copy(i):
        to = {"tensor": 1 - t}
        return remote(att_send.at[rows(i)], att_recv.at[rows(i)], att_s(i), att_r(i), to)

    def h_copies(i):
        src, dst = h2_half.at[rows(i)], h2_all.at[2 * x + t, rows(i)]
        return (
            pltpu.make_async_copy(src, dst, h_l(i)),
            remote(src, dst, hx_s(i), hx_r(i), {"x": 1 - x}),
            remote(src, dst, hy_s(i), hy_r(i), {"tensor": 1 - t}),
        )

    wo_m = merge_rows(wo_buf[...])
    for i in range(2):
        at = pl.ds(pl.multiple_of((1 - t) * half + i * quarter, quarter), quarter)
        att_send[rows(i)] = dot_nt(attn_out[at], wo_m).astype(BF)
        att_copy(i).start()
    for i in range(2):
        at = pl.ds(pl.multiple_of(t * half + i * quarter, quarter), quarter)
        mid_out[rows(i)] = dot_nt(attn_out[at], wo_m) + x_ref[at].astype(F32)
    prefetch(3)
    for i in range(2):
        att_copy(i).wait_recv()
        mid = mid_out[rows(i)] + att_recv[rows(i)].astype(F32)
        mid_out[rows(i)] = mid
        h2_half[rows(i)] = (mid * norm_factor(mid) * gain_mlp).astype(BF)
        for copy in h_copies(i):
            copy.start()
    from_side = h2_all.at[2 * (1 - x) + t, rows(0)]
    from_across = h2_all.at[2 * x + 1 - t, rows(1)]
    relay_across = remote(from_side, from_side, hyy_s(), hyy_r(), {"tensor": 1 - t})
    relay_side = remote(from_across, from_across, hxx_s(), hxx_r(), {"x": 1 - x})
    h_copies(0)[1].wait_recv()
    relay_across.start()
    dy_side(0).wait_recv()
    dy_across.start()
    prefetch(4)
    dy_side(2).start()
    h_copies(1)[2].wait_recv()
    relay_side.start()
    for tick in range(5, n1 + 3):
        prefetch(tick)

    save = pool.take(3)
    saves = [
        pltpu.make_async_copy(src, dst, save(i))
        for i, (src, dst) in enumerate(
            ((wqkv_buf, wqkv_all), (wo_buf, wo_all), (kv_buf, kv_all))
        )
    ]
    for copy in saves:
        copy.start()

    for item in (small, wqkv, wo):
        item.drain()

    def kv_drain(s, carry):
        @pl.when((s <= z) & (z < zs - 1))
        def _():
            kv_up(s).wait_send()

        @pl.when((s >= z) & (z > 0))
        def _():
            kv_dn(s).wait_send()

        @pl.when((s < z) | ((s == z) & (x == 0)))
        def _():
            kv_side(s, 0, x).wait_send()

        @pl.when((s > z) | ((s == z) & (x == 1)))
        def _():
            kv_side(s, 1, x).wait_send()

        return carry

    lax.fori_loop(0, zs, kv_drain, 0)
    relay_across.wait()
    relay_side.wait()
    dy_across.wait()
    for i in range(3):
        dy_side(i).wait_send()
        if i > 0:
            dy_side(i).wait_recv()
    for i in range(2):
        att_copy(i).wait_send()
        own, side, across = h_copies(i)
        own.wait()
        side.wait_send()
        across.wait_send()
    h_copies(1)[1].wait_recv()
    h_copies(0)[2].wait_recv()
    if n1:
        for c in range(n1):
            trade.sent(c, c)
            gather.finish(c)
            gather.drain(c)
    for copy in saves + [dy_own]:
        copy.wait()


def forward_call(
    zs, heads, n1, skip, fc, x_in, wqkv_in, wo_in, small_in, cos, sin, start, dy_in, first
):
    tok, width = x_in.shape
    half = tok // 2
    homes = 4 * zs
    rows, qkv_cols = wqkv_in.shape
    q_cols = heads * HEAD_SIZE
    shape = jax.ShapeDtypeStruct
    any_spec = pl.BlockSpec(memory_space=pl.ANY)
    out = [
        shape((tok, width), BF),
        shape((tok, q_cols), BF),
        shape((tok, q_cols), BF),
        shape((2, heads * half), F32),
        shape((half, width), F32),
        shape(small_in.shape, F32),
        shape((homes, rows, qkv_cols), BF),
        shape((homes, rows, q_cols), BF),
        shape((2 * zs + 1, half, 2 * HEAD_SIZE), BF),
        shape((4, half, width), BF),
        shape((4, half, width), BF),
    ]
    sems = [pltpu.SemaphoreType.DMA((3 * (9 * zs + 1) + 8 * zs + 3 * n1 + 36,))]
    if n1:
        out.append(shape((n1, width, 3 * fc), BF))
        sems += [pltpu.SemaphoreType.DMA((n1, zs))] * 5
    return pl.pallas_call(
        functools.partial(forward_kernel, zs, heads, n1, skip, HEAD_SIZE ** (-0.5)),
        out_shape=out,
        in_specs=[VMEM] + [any_spec] * 3 + [VMEM] * (4 + len(first)),
        out_specs=[VMEM] * 6 + [any_spec] * (len(out) - 6),
        scratch_shapes=[
            pltpu.VMEM((homes,) + small_in.shape, BF),
            pltpu.VMEM((homes, rows, qkv_cols), BF),
            pltpu.VMEM((homes, rows, q_cols), BF),
            pltpu.VMEM((2 * zs + 1, half, 2 * HEAD_SIZE), BF),
            pltpu.VMEM((2, HEAD_SIZE, heads * half), BF),
            pltpu.VMEM((2, HEAD_SIZE, heads * half), F32),
            pltpu.VMEM((2, 1, heads * half), F32),
            pltpu.VMEM((2, 1, heads * half), F32),
            pltpu.VMEM((half, width), BF),
            pltpu.VMEM((half, width), BF),
            pltpu.VMEM((half, width), BF),
            pltpu.VMEM((tok, width), F32),
        ]
        + sems,
        compiler_params=pltpu.CompilerParams(
            collective_id=1, has_side_effects=True, vmem_limit_bytes=60 * 2**20
        ),
        cost_estimate=pl.CostEstimate(
            flops=2 * tok * width * (qkv_cols + q_cols) + 2**31,
            bytes_accessed=32 * 2**20,
            transcendentals=0,
        ),
    )(x_in, wqkv_in, wo_in, small_in, cos, sin, start, dy_in, *first)


class Square:
    def __init__(self, src, own, r_one, r_two, pool):
        self.src, self.own, self.r_one, self.r_two = src, own, r_one, r_two
        self.x, self.t = lax.axis_index("x"), lax.axis_index("tensor")
        self.cut = src.shape[2] // 2
        self.one_s, self.one_r = pool.take(3), pool.take(3)
        self.two_s, self.two_r = pool.take(2), pool.take(2)
        self.load = pool.take(3)

    def first(self):
        x, t, cut, src = self.x, self.t, self.cut, self.src
        left, right = pl.ds(0, cut), pl.ds(cut, cut)
        sends = [
            remote(
                src.at[pl.ds(2 * (1 - x), 2), :, left],
                self.r_one.at[pl.ds(0, 2)],
                self.one_s(0),
                self.one_r(0),
                {"x": 1 - x},
            )
        ]
        for i in range(2):
            sends.append(
                remote(
                    src.at[2 * i + 1 - t, :, right],
                    self.r_one.at[2 + i],
                    self.one_s(1 + i),
                    self.one_r(1 + i),
                    {"tensor": 1 - t},
                )
            )
        return sends

    def loads(self):
        x, t, cut, src = self.x, self.t, self.cut, self.src
        left, right = pl.ds(0, cut), pl.ds(cut, cut)
        loads = [
            pltpu.make_async_copy(
                src.at[pl.ds(2 * x, 2), :, left], self.own.at[pl.ds(0, 2)], self.load(0)
            )
        ]
        for i in range(2):
            loads.append(
                pltpu.make_async_copy(
                    src.at[2 * i + t, :, right], self.own.at[2 + i], self.load(1 + i)
                )
            )
        return loads

    def second(self):
        x, t = self.x, self.t
        return [
            remote(
                self.own.at[1 - t],
                self.r_two.at[0],
                self.two_s(0),
                self.two_r(0),
                {"tensor": 1 - t},
            ),
            remote(
                self.own.at[3 - x],
                self.r_two.at[1],
                self.two_s(1),
                self.two_r(1),
                {"x": 1 - x},
            ),
        ]

    def start(self):
        for copy in self.first() + self.loads():
            copy.start()

    def turn(self):
        for copy in self.loads():
            copy.wait()
        for copy in self.first():
            copy.wait_recv()
        for i in range(4):
            self.own[i] = (self.own[i].astype(F32) + self.r_one[i].astype(F32)).astype(BF)
        for copy in self.second():
            copy.start()

    def result(self):
        for copy in self.second():
            copy.wait_recv()
        left = self.own[self.t].astype(F32) + self.r_two[0].astype(F32)
        right = self.own[2 + self.x].astype(F32) + self.r_two[1].astype(F32)
        return jnp.concatenate([left, right], axis=1)

    def drain(self):
        for copy in self.first() + self.second():
            copy.wait_send()


class Collect:
    def __init__(self, zs, acc, to_sib, r_sib, r_x, r_z, out, pool):
        self.zs, self.acc, self.to_sib, self.r_sib = zs, acc, to_sib, r_sib
        self.r_x, self.r_z, self.out = r_x, r_z, out
        self.b, self.z, self.x = (lax.axis_index(a) for a in ("batch", "z", "x"))
        self.s_s, self.s_r, self.x_s, self.x_r, self.loc = (pool.take() for _ in range(5))
        self.d_s, self.d_r, self.u_s, self.u_r = (pool.take(zs) for _ in range(4))

    def sib(self):
        return remote(self.to_sib, self.r_sib, self.s_s(), self.s_r(), {"batch": 1 - self.b})

    def side(self):
        return remote(
            self.acc.at[1 - self.x], self.r_x, self.x_s(), self.x_r(), {"x": 1 - self.x}
        )

    def dn(self, h):
        return remote(
            self.acc.at[self.x, h], self.r_z.at[h], self.d_s(h), self.d_r(h), {"z": self.z - 1}
        )

    def up(self, h):
        return remote(
            self.acc.at[self.x, h], self.r_z.at[h + 1], self.u_s(h), self.u_r(h), {"z": self.z + 1}
        )

    def fill(self, make):
        rows = self.acc.shape[2]
        for buf, core in ((self.to_sib, 1 - self.b), (self.acc, self.b)):
            value = make(core)
            for h in range(self.zs):
                for col in range(2):
                    i = 2 * h + col
                    buf[col, h] = value[i * rows : (i + 1) * rows].astype(BF)
            if buf is self.to_sib:
                self.sib().start()

    def add(self, dst, src):
        dst[...] = (dst[...].astype(F32) + src[...].astype(F32)).astype(BF)

    def after_sib(self):
        self.sib().wait_recv()

        def one(h, carry):
            self.add(self.acc.at[1 - self.x, h], self.r_sib.at[1 - self.x, h])
            return carry

        lax.fori_loop(0, self.zs, one, 0)
        self.side().start()

        def other(h, carry):
            self.add(self.acc.at[self.x, h], self.r_sib.at[self.x, h])
            return carry

        lax.fori_loop(0, self.zs, other, 0)

    def after_side(self):
        self.side().wait_recv()

        def one(h, carry):
            self.add(self.acc.at[self.x, h], self.r_x.at[h])
            return carry

        lax.fori_loop(0, self.zs, one, 0)

        def ends(h, carry):
            @pl.when((self.z == self.zs - 1) & (h < self.z))
            def _():
                self.dn(h).start()

            @pl.when((self.z == 0) & (h > 0))
            def _():
                self.up(h).start()

            return carry

        lax.fori_loop(0, self.zs, ends, 0)

    def step(self, k):
        def one(i, carry):
            @pl.when((self.z == self.zs - 1 - k) & (i <= self.z))
            def _():
                self.dn(i).wait_recv()
                self.add(self.acc.at[self.x, i], self.r_z.at[i])

                @pl.when(i < self.z)
                def _():
                    self.dn(i).start()

            j = self.zs - 1 - i

            @pl.when((self.z == k) & (j >= self.z))
            def _():
                self.up(j).wait_recv()
                self.add(self.acc.at[self.x, j], self.r_z.at[j + 1])

                @pl.when(j > self.z)
                def _():
                    self.up(j).start()

            return carry

        lax.fori_loop(0, self.zs, one, 0)
        if k == self.zs - 1:
            self.result().start()

    def result(self):
        return pltpu.make_async_copy(self.acc.at[self.x, self.z], self.out, self.loc())

    def drain(self):
        self.sib().wait_send()
        self.side().wait_send()
        self.result().wait()

        def one(h, carry):
            @pl.when(h < self.z)
            def _():
                self.dn(h).wait_send()

            @pl.when(h > self.z)
            def _():
                self.up(h).wait_send()

            return carry

        lax.fori_loop(0, self.zs, one, 0)


class LineSum:
    def __init__(self, zs, acc, r_z, pool):
        self.zs, self.acc, self.r_z = zs, acc, r_z
        self.z = lax.axis_index("z")
        self.d_s, self.d_r, self.u_s, self.u_r = (pool.take(zs) for _ in range(4))

    def dn(self, h):
        to = {"z": self.z - 1}
        return remote(self.acc.at[:, h], self.r_z.at[:, h], self.d_s(h), self.d_r(h), to)

    def up(self, h):
        to = {"z": self.z + 1}
        return remote(self.acc.at[:, h], self.r_z.at[:, h + 1], self.u_s(h), self.u_r(h), to)

    def start(self):
        for h in range(self.zs):
            if h < self.zs - 1:

                @pl.when(self.z == self.zs - 1)
                def _():
                    self.dn(h).start()

            if h > 0:

                @pl.when(self.z == 0)
                def _():
                    self.up(self.zs - h).start()

    def plus(self, h, slot):
        for c in range(self.acc.shape[0]):
            total = self.acc[c, h].astype(F32) + self.r_z[c, slot].astype(F32)
            self.acc[c, h] = total.astype(BF)

    def step(self, k):
        def one(i, carry):
            @pl.when((self.z == self.zs - 1 - k) & (i <= self.z))
            def _():
                self.dn(i).wait_recv()
                self.plus(i, i)

                @pl.when(i < self.z)
                def _():
                    self.dn(i).start()

            j = self.zs - 1 - i

            @pl.when((self.z == k) & (j >= self.z))
            def _():
                self.up(j).wait_recv()
                self.plus(j, j + 1)

                @pl.when(j > self.z)
                def _():
                    self.up(j).start()

            return carry

        lax.fori_loop(0, self.zs, one, 0)

    def drain(self):
        def one(h, carry):
            @pl.when(h < self.z)
            def _():
                self.dn(h).wait_send()

            @pl.when(h > self.z)
            def _():
                self.up(h).wait_send()

            return carry

        lax.fori_loop(0, self.zs, one, 0)


def backward_kernel(zs, heads, nl, scale, *refs):
    refs = list(refs)

    def take(count):
        out = refs[:count]
        del refs[:count]
        return out

    y_in, g_mlp = take(2)
    if nl:
        (left_in,) = take(1)
    dh2_ref, mid_ref, vec_ref, x_ref, dy_ref, h1_ref, q_ref, attn_ref, lse_ref, kv_ref = take(10)
    wqkv_ref, wo_ref, cos_ref, sin_ref, start_ref = take(5)
    out_all, gh_all, g_q, g_kv, g_wo, g_vec, g_far = take(7)
    if nl:
        (left_out,) = take(1)
    y_own, y_one, y_two, dmid_ref, dat_ref, half_ref = take(6)
    q_s, do_s, q_t, do_t, delta_ref = take(5)
    dkv_ref, rx_ref, rz_ref, acc_ref, dqkv_ref, dh_send, dh_recv = take(7)
    bufs_q, bufs_kv, bufs_wo = take(5), take(5), take(5)
    vec_own, vec_recv, vec_z, sem_ref = take(4)
    if nl:
        left_acc, left_z = take(2)

    b, z, x, t = (lax.axis_index(a) for a in ("batch", "z", "x", "tensor"))
    shards = 2 * zs
    me = 2 * z + x
    half, width = mid_ref.shape
    q_cols = heads * HEAD_SIZE
    pool = Pool(sem_ref)
    greet(z, zs)

    sq_y = Square(y_in, y_own, y_one, y_two, pool)
    col_q = Collect(zs, *bufs_q, g_q, pool)
    col_kv = Collect(zs, *bufs_kv, g_kv, pool)
    col_wo = Collect(zs, *bufs_wo, g_wo, pool)
    runs = thirds(zs)
    if nl:
        lines = [
            LineSum(zs, left_acc.at[pl.ds(c, 1)], left_z.at[pl.ds(c, 1)], pool) for c in range(nl)
        ]
        left_l = pool.take()
        left_load = pltpu.make_async_copy(left_in, left_acc, left_l())
        left_load.start()

    def line_tick(tick):
        for c in range(nl):
            if tick == c:
                lines[c].start()
            for k in range(1, zs):
                if min(k, 3) == tick - c:
                    lines[c].step(k)

    vec = vec_ref[...]
    gain_attn = lanes(vec, 4, 6)
    gain_mlp = lanes(vec, 10, 6)

    mid = mid_ref[...]
    d_norm, g_norm_mlp = norm_backward(mid, norm_factor(mid), gain_mlp, dh2_ref[...])
    mine = pl.ds(pl.multiple_of(t * half, half), half)
    dmid_ref[...] = dy_ref[mine].astype(F32) + d_norm
    dat_ref[t] = dmid_ref[...].astype(BF)
    dat_s, dat_r = pool.take(), pool.take()

    def dat_copy(i):
        return remote(dat_ref.at[i], dat_ref.at[i], dat_s(), dat_r(), {"tensor": 1 - t})

    dat_copy(t).start()
    if nl:
        left_load.wait()
        line_tick(0)

    x0_s, x0_r, x1_s, x1_r = (pool.take(zs) for _ in range(4))
    c0_s, c0_r, c1_s, c1_r = (pool.take(zs) for _ in range(4))

    def side(s, sub):
        src = dkv_ref.at[2 * s + 1 - x + sub]
        send, recv = (x0_s, x0_r) if sub == 0 else (x1_s, x1_r)
        return remote(src, rx_ref.at[s + sub], send(s), recv(s), {"x": 1 - x})

    def chain(s, sub):
        src = dkv_ref.at[2 * s + x + sub]
        send, recv = (c0_s, c0_r) if sub == 0 else (c1_s, c1_r)
        to = z - 1 if sub == 0 else z + 1
        return remote(src, rz_ref.at[s + sub], send(s), recv(s), {"z": to})

    acc_ref[...] = jnp.zeros_like(acc_ref)

    def prepare(sub):
        d_out = dot(dat_ref[sub], merge_rows(wo_ref[...])).astype(BF)
        rows = pl.ds(pl.multiple_of(sub * half, half), half)
        out = attn_ref[rows]
        q = q_ref[rows]
        for h in range(heads):
            cols = slice(h * HEAD_SIZE, (h + 1) * HEAD_SIZE)
            at = slice(h * half, (h + 1) * half)
            q_s[sub, at] = q[:, cols]
            do_s[sub, at] = d_out[:, cols]
            q_t[sub, :, at] = q[:, cols].T
            do_h = d_out[:, cols].T
            do_t[sub, :, at] = do_h
            delta_ref[sub, :, at] = jnp.sum(
                do_h.astype(F32) * out[:, cols].T.astype(F32), axis=0, keepdims=True
            )

    def fold(sub, block):
        slot = block + sub
        keys = kv_ref[slot, :, :HEAD_SIZE]
        vals = kv_ref[slot, :, HEAD_SIZE:]
        scores = dot(keys, q_t[sub]) * scale + block_mask(
            sub, block, me, shards, half, start_ref[sub], heads
        )
        probs = jnp.exp(scores - lse_ref[sub])
        d_scores = (probs * (dot(vals, do_t[sub]) - delta_ref[sub])).astype(BF)
        dkv_ref[slot, :, HEAD_SIZE:] = dot(probs.astype(BF), do_s[sub]).astype(BF)
        dkv_ref[slot, :, :HEAD_SIZE] = (dot(d_scores, q_s[sub]) * scale).astype(BF)
        acc_ref[sub] += dot(keys.T, d_scores)

    def far_blocks(sub):
        def one(k, carry):
            s = jnp.where(sub == 0, z - k, z + k)

            @pl.when(in_range(s, zs) & ((k > 0) | (x != sub)))
            def _():
                fold(sub, 2 * s + 1 - x)

                @pl.when(sub == 0)
                def _():
                    side(s, 0).start()

                @pl.when(sub == 1)
                def _():
                    side(s, 1).start()

            return carry

        lax.fori_loop(0, zs, one, 0)

    def near_blocks(sub):
        def one(i, carry):
            k = zs - 1 - i
            s = jnp.where(sub == 0, z - k, z + k)

            @pl.when(in_range(s, zs))
            def _():
                fold(sub, 2 * s + x)

            return carry

        lax.fori_loop(0, zs, one, 0)

    def tokens(i, carry):
        sub = jnp.where(i == 0, t, 1 - t)

        @pl.when(i == 1)
        def _():
            line_tick(1)
            dat_copy(1 - t).wait_recv()

        prepare(sub)
        far_blocks(sub)
        near_blocks(sub)
        return carry

    lax.fori_loop(0, 2, tokens, 0)
    sq_y.start()

    def wo_part(core):
        rows = width // 2
        at = pl.ds(pl.multiple_of(core * rows, rows), rows)
        return dot(half_ref[at], attn_ref[...])

    def plus(slot, src):
        total = dkv_ref[slot].astype(F32) + src[...].astype(F32)
        dkv_ref[slot] = total.astype(BF)

    def kv_begin():
        def one(i, carry):
            j = zs - 1 - i

            @pl.when((i < z) | ((i == z) & (x == 0)))
            def _():
                side(i, 0).wait_recv()
                plus(2 * i + x, rx_ref.at[i])

            @pl.when((z == zs - 1) & (i < z))
            def _():
                chain(i, 0).start()

            @pl.when((j > z) | ((j == z) & (x == 1)))
            def _():
                side(j, 1).wait_recv()
                plus(2 * j + x + 1, rx_ref.at[j + 1])

            @pl.when((z == 0) & (j > z))
            def _():
                chain(j, 1).start()

            return carry

        lax.fori_loop(0, zs, one, 0)

    def kv_step(k):
        def one(i, carry):
            j = zs - 1 - i

            @pl.when((z == zs - 1 - k) & (i <= z))
            def _():
                chain(i, 0).wait_recv()
                plus(2 * i + x, rz_ref.at[i])

                @pl.when(i < z)
                def _():
                    chain(i, 0).start()

            @pl.when((z == k) & (j >= z))
            def _():
                chain(j, 1).wait_recv()
                plus(2 * j + x + 1, rz_ref.at[j + 1])

                @pl.when(j > z)
                def _():
                    chain(j, 1).start()

            return carry

        lax.fori_loop(0, zs, one, 0)

    kv_begin()
    for i in range(2):
        half_ref[:, i * half : (i + 1) * half] = dat_ref[i].T
    col_wo.fill(wo_part)


    def back(v, at):
        return v * cos_ref[at] - pltpu.roll(v, HEAD_SIZE // 2, 1) * sin_ref[at]

    for sub in range(2):
        at = slice(sub * half, (sub + 1) * half)
        for h in range(heads):
            v = acc_ref[sub, :, h * half : (h + 1) * half].T * scale
            dqkv_ref[at, h * HEAD_SIZE : (h + 1) * HEAD_SIZE] = back(v, at).astype(BF)
    half_ref[...] = h1_ref[...].T
    col_wo.after_sib()
    for k in runs[0]:
        kv_step(k)

    def part(first, last):
        def make(core):
            rows = width // 2
            at = pl.ds(pl.multiple_of(core * rows, rows), rows)
            return dot(half_ref[at], dqkv_ref[:, first:last])

        return make

    col_q.fill(part(0, q_cols))
    for k in runs[1]:
        kv_step(k)
    line_tick(2)
    for k in runs[2]:
        kv_step(k)
    for sub in range(2):
        at = slice(sub * half, (sub + 1) * half)
        dk = dkv_ref[me + sub, :, :HEAD_SIZE].astype(F32)
        dqkv_ref[at, q_cols : q_cols + HEAD_SIZE] = back(dk, at).astype(BF)
        dqkv_ref[at, q_cols + HEAD_SIZE :] = dkv_ref[me + sub, :, HEAD_SIZE:]

    dh_s, dh_r = pool.take(), pool.take()
    dh_copy = remote(dh_send, dh_recv, dh_s(), dh_r(), {"tensor": 1 - t})
    theirs = pl.ds(pl.multiple_of((1 - t) * half, half), half)
    own = pl.ds(pl.multiple_of(t * half, half), half)
    dh_send[...] = dot_nt(dqkv_ref[theirs], merge_rows(wqkv_ref[...])).astype(BF)
    dh_copy.start()
    col_kv.fill(part(q_cols, q_cols + 2 * HEAD_SIZE))
    dh1 = dot_nt(dqkv_ref[own], merge_rows(wqkv_ref[...]))
    col_q.after_sib()
    col_kv.after_sib()
    col_wo.after_side()
    sq_y.turn()
    line_tick(3)

    dh_copy.wait_recv()
    dh1 = dh1 + dh_recv[...].astype(F32)
    xv = x_ref[mine].astype(F32)
    d_norm, g_norm_attn = norm_backward(xv, norm_factor(xv), gain_attn, dh1)

    g_bias = jnp.sum(dqkv_ref[...].astype(F32), axis=0, keepdims=True)
    row = jnp.concatenate([g_bias, g_norm_attn, g_norm_mlp], axis=1)
    lane = vec_ref.shape[1]
    vec_own[...] = jnp.concatenate(
        [row[:, i * lane : (i + 1) * lane] for i in range(vec_ref.shape[0])], axis=0
    )
    v_s, v_r = pool.take(3), pool.take(3)
    vz_s, vz_r = pool.take(zs), pool.take(zs)
    norms = (lax.broadcasted_iota(jnp.int32, vec_ref.shape, 0) >= 4).astype(F32)

    def v_side(i):
        axis, index = (("tensor", t), ("x", x), ("batch", b))[i]
        return remote(vec_own, vec_recv.at[i], v_s(i), v_r(i), {axis: 1 - index})

    def v_add(i):
        v_side(i).wait()
        other = vec_recv[i]
        vec_own[...] = vec_own[...] + (other * norms if i == 0 else other)

    v_side(0).start()
    dat_copy(t).wait_send()
    dat_ref[t] = (dmid_ref[...] + d_norm).astype(BF)
    gh_s, gh_r, gh_l = (pool.take() for _ in range(3))
    gh_copy = remote(dat_ref.at[t], gh_all.at[t], gh_s(), gh_r(), {"tensor": 1 - t})
    gh_own = pltpu.make_async_copy(dat_ref.at[t], gh_all.at[t], gh_l())
    gh_copy.start()
    gh_own.start()
    line_tick(4)
    v_add(0)
    v_side(1).start()
    far_s, far_r = pool.take(), pool.take()
    far_copy = remote(
        g_mlp.at[:, 1 - x],
        g_far.at[pl.ds(0, g_mlp.shape[0])],
        far_s(),
        far_r(),
        {"x": 1 - x},
    )
    far_copy.start()
    col_kv.after_side()
    for k in runs[0]:
        col_wo.step(k)
    if nl:
        for tick in range(5, nl + 3):
            line_tick(tick)
    for k in runs[0]:
        col_kv.step(k)
    v_add(1)
    v_side(2).start()
    y_sum = sq_y.result()
    sq_y.drain()
    total = mid_ref[...] + y_sum
    cut = width // 2
    o_s, o_r, o_l = pool.take(2), pool.take(2), pool.take(2)
    sends, locals_ = [], []
    for i in range(2):
        y_own[i] = total[:, i * cut : (i + 1) * cut].astype(BF)
        dst = out_all.at[t, :, pl.ds(i * cut, cut)]
        sends.append(remote(y_own.at[i], dst, o_s(i), o_r(i), {"tensor": 1 - t}))
        locals_.append(pltpu.make_async_copy(y_own.at[i], dst, o_l(i)))
    for copy in sends + locals_:
        copy.start()
    for k in runs[1]:
        col_wo.step(k)
    col_q.after_side()
    if nl:
        lf_s, lf_r, lf_l = (pool.take() for _ in range(3))
        rows = g_far.shape[1]

        def left_rows(col):
            return left_acc.at[:, z, pl.ds(pl.multiple_of(col * rows, rows), rows)]

        left_far = remote(
            left_rows(1 - x),
            g_far.at[pl.ds(g_mlp.shape[0], nl)],
            lf_s(),
            lf_r(),
            {"x": 1 - x},
        )
        left_own = pltpu.make_async_copy(left_rows(x), left_out, lf_l())
        left_far.start()
        left_own.start()
    for k in runs[2]:
        col_wo.step(k)
    v_add(2)

    def v_copy(to):
        return remote(vec_own, vec_z.at[z], vz_s(to), vz_r(z), {"z": to})

    for to in range(zs):

        @pl.when(to != z)
        def _():
            v_copy(to).start()

    for k in runs[1]:
        col_kv.step(k)
    for run in runs:
        for k in run:
            col_q.step(k)
    for k in runs[2]:
        col_kv.step(k)
    total = jnp.zeros(vec_ref.shape, F32)
    for frm in range(zs):

        @pl.when(frm != z)
        def _():
            remote(vec_own, vec_z.at[frm], vz_s(frm), vz_r(frm), {"z": frm}).wait_recv()

        @pl.when(frm == z)
        def _():
            vec_z[frm] = vec_own[...]

        total = total + vec_z[frm]
    g_vec[...] = total

    for to in range(zs):

        @pl.when(to != z)
        def _():
            v_copy(to).wait_send()

    def dkv_drain(s, carry):
        @pl.when((s < z) | ((s == z) & (x == 1)))
        def _():
            side(s, 0).wait_send()

        @pl.when((s > z) | ((s == z) & (x == 0)))
        def _():
            side(s, 1).wait_send()

        @pl.when(s < z)
        def _():
            chain(s, 0).wait_send()

        @pl.when(s > z)
        def _():
            chain(s, 1).wait_send()

        return carry

    lax.fori_loop(0, zs, dkv_drain, 0)
    for item in (col_wo, col_q, col_kv):
        item.drain()
    dh_copy.wait_send()
    far_copy.wait()
    gh_own.wait()
    gh_copy.wait()
    for copy in sends + locals_:
        copy.wait()
    if nl:
        for item in lines:
            item.drain()
        left_far.wait()
        left_own.wait()


def backward_call(zs, heads, left, big, small):
    mid, vec = small[1:3]
    wqkv = small[10]
    half, width = mid.shape
    tok = 2 * half
    _, rows, qkv_cols = wqkv.shape
    q_cols = heads * HEAD_SIZE
    n2, _, _, three = big[1].shape
    nl = left[0].shape[0] if left else 0
    shape = jax.ShapeDtypeStruct
    any_spec = pl.BlockSpec(memory_space=pl.ANY)
    vm = pltpu.VMEM
    cut = width // 2

    def collect(cols):
        return [
            vm((2, zs, rows, cols), BF),
            vm((2, zs, rows, cols), BF),
            vm((2, zs, rows, cols), BF),
            vm((zs, rows, cols), BF),
            vm((zs + 1, rows, cols), BF),
        ]

    square = [vm((4, half, cut), BF), vm((4, half, cut), BF), vm((2, half, cut), BF)]
    lines = [vm(left[0].shape, BF), vm((nl, zs + 1) + left[0].shape[2:], BF)] if nl else []
    return pl.pallas_call(
        functools.partial(backward_kernel, zs, heads, nl, HEAD_SIZE ** (-0.5)),
        out_shape=[
            shape((2, half, width), BF),
            shape((2, half, width), BF),
            shape((rows, q_cols), BF),
            shape((rows, 2 * HEAD_SIZE), BF),
            shape((rows, q_cols), BF),
            shape(vec.shape, F32),
            shape((n2 + nl, rows, three), BF),
        ]
        + ([shape((nl, rows, three), BF)] if nl else []),
        in_specs=[any_spec] * (2 + len(left)) + [VMEM] * len(small),
        out_specs=[any_spec] * 5 + [VMEM, any_spec] + [any_spec] * len(left),
        scratch_shapes=square
        + [
            vm((half, width), F32),
            vm((2, half, width), BF),
            vm((width, tok), BF),
            vm((2, heads * half, HEAD_SIZE), BF),
            vm((2, heads * half, HEAD_SIZE), BF),
            vm((2, HEAD_SIZE, heads * half), BF),
            vm((2, HEAD_SIZE, heads * half), BF),
            vm((2, 1, heads * half), F32),
            vm((2 * zs + 1, half, 2 * HEAD_SIZE), BF),
            vm((zs + 1, half, 2 * HEAD_SIZE), BF),
            vm((zs + 1, half, 2 * HEAD_SIZE), BF),
            vm((2, HEAD_SIZE, heads * half), F32),
            vm((tok, qkv_cols), BF),
            vm((half, width), BF),
            vm((half, width), BF),
        ]
        + collect(q_cols)
        + collect(2 * HEAD_SIZE)
        + collect(q_cols)
        + [
            vm(vec.shape, F32),
            vm((3,) + vec.shape, F32),
            vm((zs,) + vec.shape, F32),
            pltpu.SemaphoreType.DMA(((22 + 4 * nl) * zs + 90,)),
        ]
        + lines,
        compiler_params=pltpu.CompilerParams(
            collective_id=2, has_side_effects=True, vmem_limit_bytes=63 * 2**20
        ),
        cost_estimate=pl.CostEstimate(
            flops=4 * tok * width * (qkv_cols + q_cols) + 2**32,
            bytes_accessed=32 * 2**20,
            transcendentals=0,
        ),
    )(*big, *left, *small)


def remote(src, dst, send, recv, to):
    return pltpu.make_async_remote_copy(
        src_ref=src,
        dst_ref=dst,
        send_sem=send,
        recv_sem=recv,
        device_id=to,
        device_id_type=pl.DeviceIdType.MESH,
    )


def greet(z, zs):
    barrier = pltpu.get_barrier_semaphore()
    for axis in ("batch", "x", "tensor"):
        other = {axis: 1 - lax.axis_index(axis)}
        pl.semaphore_signal(barrier, inc=1, device_id=other, device_id_type=pl.DeviceIdType.MESH)

    @pl.when(z > 0)
    def _():
        pl.semaphore_signal(
            barrier, inc=1, device_id={"z": z - 1}, device_id_type=pl.DeviceIdType.MESH
        )

    @pl.when(z < zs - 1)
    def _():
        pl.semaphore_signal(
            barrier, inc=1, device_id={"z": z + 1}, device_id_type=pl.DeviceIdType.MESH
        )

    pl.semaphore_wait(barrier, 5 - (z == 0).astype(jnp.int32) - (z == zs - 1).astype(jnp.int32))


def in_range(c, count):
    return (c >= 0) & (c < count)


class Exchange:
    def __init__(self, mats, full, first, zs, skip, sems):
        self.mats, self.full, self.first = mats, full, first
        self.x = lax.axis_index("x")
        home = (lax.axis_index("batch") * zs + lax.axis_index("z")) * 2 + self.x
        self.rows, self.cols = mats[0].shape[0], full.shape[2] // 3
        self.at = pl.ds(pl.multiple_of(home * self.rows, self.rows), self.rows)
        self.shift = mats[0].shape[1] // 2 - skip // 2
        self.send, self.recv, self.loc = sems

    def pieces(self, c):
        for w, mat in enumerate(self.mats):
            dst = self.full.at[c, self.at, pl.ds(w * self.cols, self.cols)]
            yield mat, dst

    def source(self, mat, c, x):
        first = pl.multiple_of(x * self.shift + (self.first + c) * self.cols, 128)
        return mat.at[:, pl.ds(first, self.cols)]

    def ship(self, c, i):
        for mat, dst in self.pieces(c):
            src = self.source(mat, c, 1 - self.x)
            remote(src, dst, self.send(i), self.recv(i), {"x": 1 - self.x}).start()

    def keep(self, c, i):
        for mat, dst in self.pieces(c):
            pltpu.make_async_copy(self.source(mat, c, self.x), dst, self.loc(i)).start()

    def fetch(self, c, other, buf, sem):
        x = 1 - self.x if other else self.x
        for w, mat in enumerate(self.mats):
            dst = buf.at[pl.ds(c * self.rows, self.rows), pl.ds(w * self.cols, self.cols)]
            pltpu.make_async_copy(self.source(mat, c, x), dst, sem).start()

    def both(self, c, i):
        spot = self.full.at[c, self.at]
        return remote(spot, spot, self.send(i), self.recv(i), {"x": 1 - self.x})

    def arrived(self, c, i):
        self.both(c, i).wait_recv()
        spot = self.full.at[c, self.at]
        pltpu.make_async_copy(spot, spot, self.loc(i)).wait()

    def sent(self, c, i):
        self.both(c, i).wait_send()


class Gather:
    def __init__(self, zs, mine, full, sems):
        self.zs, self.mine, self.full = zs, mine, full
        self.loc, self.up, self.dn, self.zr, self.ss, self.sr = sems
        self.b, self.z = lax.axis_index("batch"), lax.axis_index("z")
        self.size = full.shape[1] // (2 * zs)

    def at(self, c, b, z):
        rows = pl.ds(pl.multiple_of((b * self.zs + z) * self.size, self.size), self.size)
        return self.full.at[:, rows] if c is None else self.full.at[c, rows]

    def sems(self, c, s):
        i = 0 if c is None else c
        return (ref.at[i, s] for ref in (self.up, self.dn, self.zr, self.ss, self.sr))

    def up_copy(self, c, s, src=None):
        dst = self.at(c, self.b, s)
        up, _, zr, _, _ = self.sems(c, s)
        return remote(dst if src is None else src, dst, up, zr, {"z": self.z + 1})

    def dn_copy(self, c, s, src=None):
        dst = self.at(c, self.b, s)
        _, dn, zr, _, _ = self.sems(c, s)
        return remote(dst if src is None else src, dst, dn, zr, {"z": self.z - 1})

    def sib_copy(self, c, s, src=None):
        dst = self.at(c, self.b, s)
        _, _, _, ss, sr = self.sems(c, s)
        return remote(dst if src is None else src, dst, ss, sr, {"batch": 1 - self.b})

    def local(self, c):
        return pltpu.make_async_copy(self.mine.at[c], self.at(c, self.b, self.z), self.loc.at[c])

    def start(self, c):
        src = None if self.mine is None else self.mine.at[c]

        @pl.when(self.z < self.zs - 1)
        def _():
            self.up_copy(c, self.z, src).start()

        @pl.when(self.z > 0)
        def _():
            self.dn_copy(c, self.z, src).start()

        self.sib_copy(c, self.z, src).start()
        if self.mine is not None:
            self.local(c).start()

    def hop(self, c, k):
        low, high = self.z - k, self.z + k

        @pl.when(low >= 0)
        def _():
            self.dn_copy(c, low).wait_recv()

            @pl.when(self.z < self.zs - 1)
            def _():
                self.up_copy(c, low).start()

            self.sib_copy(c, low).start()

        @pl.when(high < self.zs)
        def _():
            self.dn_copy(c, high).wait_recv()

            @pl.when(self.z > 0)
            def _():
                self.dn_copy(c, high).start()

            self.sib_copy(c, high).start()

    def finish(self, c):
        if self.mine is not None:
            self.local(c).wait()
        for s in range(self.zs):
            dst = self.at(c, 1 - self.b, s)
            _, _, _, ss, sr = self.sems(c, s)
            remote(dst, dst, ss, sr, {"batch": 1 - self.b}).wait_recv()

    def drain(self, c):
        for s in range(self.zs):

            @pl.when((s <= self.z) & (self.z < self.zs - 1))
            def _():
                self.up_copy(c, s).wait_send()

            @pl.when((s >= self.z) & (self.z > 0))
            def _():
                self.dn_copy(c, s).wait_send()

            self.sib_copy(c, s).wait_send()


class Reduce:
    def __init__(self, zs, ends, ring, to_sib, r_sib, r_dn, r_up, tmp, out, left, sems):
        self.zs, self.ring, self.to_sib, self.out = zs, ring, to_sib, out
        self.ends, self.left = ends, left
        self.r_sib, self.r_dn, self.r_up = r_sib, r_dn, r_up
        self.tmp_s, self.tmp_d, self.tmp_u = tmp
        self.s_s, self.s_r, self.d_s, self.d_r, self.u_s, self.u_r, self.load, self.o_s, self.l_s = sems
        self.b, self.z = lax.axis_index("batch"), lax.axis_index("z")
        self.slots = ring.shape[0]
        self.size = ring.shape[1] // zs

    def rows(self, h):
        return pl.ds(pl.multiple_of(h * self.size, self.size), self.size)

    def sib(self, c):
        return remote(
            self.to_sib, self.r_sib.at[c], self.s_s.at[c], self.s_r.at[c], {"batch": 1 - self.b}
        )

    def dn(self, c, h):
        src = self.ring.at[lax.rem(c, self.slots), self.rows(h)]
        dst = self.r_dn.at[c, self.rows(h)]
        return remote(src, dst, self.d_s.at[c, h], self.d_r.at[c, h], {"z": self.z - 1})

    def up(self, c, h):
        src = self.ring.at[lax.rem(c, self.slots), self.rows(h)]
        dst = self.r_up.at[c, self.rows(h)]
        return remote(src, dst, self.u_s.at[c, h], self.u_r.at[c, h], {"z": self.z + 1})

    def load_sib(self, c):
        return pltpu.make_async_copy(self.r_sib.at[c], self.tmp_s, self.load.at[0])

    def load_dn(self, c, h):
        rows = self.rows(h)
        return pltpu.make_async_copy(self.r_dn.at[c, rows], self.tmp_d.at[rows], self.load.at[1 + h])

    def load_up(self, c, h):
        rows = self.rows(h)
        return pltpu.make_async_copy(
            self.r_up.at[c, rows], self.tmp_u.at[rows], self.load.at[1 + self.zs + h]
        )

    def arrive(self, c_sib, c_dn, c_up, count):
        @pl.when(in_range(c_sib, count))
        def _():
            self.sib(c_sib).wait_recv()
            self.load_sib(c_sib).start()

        for h in range(self.zs):

            @pl.when(in_range(c_dn, self.ends) & (self.z < self.zs - 1) & (h <= self.z))
            def _():
                self.dn(c_dn, h).wait_recv()
                self.load_dn(c_dn, h).start()

            @pl.when(in_range(c_up, self.ends) & (self.z > 0) & (h >= self.z))
            def _():
                self.up(c_up, h).wait_recv()
                self.load_up(c_up, h).start()

    def add(self, slot, rows, tmp):
        total = self.ring[slot, rows].astype(F32) + tmp[rows].astype(F32)
        self.ring[slot, rows] = total.astype(BF)

    def pass_on(self, c_sib, c_dn, c_up, count):
        @pl.when(in_range(c_sib, count))
        def _():
            self.load_sib(c_sib).wait()
            slot = lax.rem(c_sib, self.slots)
            for h in range(self.zs):
                self.add(slot, pl.ds(h * self.size, self.size), self.tmp_s)
            for h in range(self.zs - 1):

                @pl.when((self.z == self.zs - 1) & (c_sib < self.ends))
                def _():
                    self.dn(c_sib, h).start()

            for h in range(1, self.zs):

                @pl.when((self.z == 0) & (c_sib < self.ends))
                def _():
                    self.up(c_sib, h).start()

            if self.left is not None:

                @pl.when(c_sib >= self.ends)
                def _():
                    self.leave(c_sib).start()

        for h in range(self.zs):

            @pl.when(in_range(c_dn, self.ends) & (self.z < self.zs - 1) & (h <= self.z))
            def _():
                self.load_dn(c_dn, h).wait()
                self.add(lax.rem(c_dn, self.slots), pl.ds(h * self.size, self.size), self.tmp_d)

                @pl.when(h < self.z)
                def _():
                    self.dn(c_dn, h).start()

            @pl.when(in_range(c_up, self.ends) & (self.z > 0) & (h >= self.z))
            def _():
                self.load_up(c_up, h).wait()
                self.add(lax.rem(c_up, self.slots), pl.ds(h * self.size, self.size), self.tmp_u)

                @pl.when(h > self.z)
                def _():
                    self.up(c_up, h).start()

    def leave(self, c):
        src = self.ring.at[lax.rem(c, self.slots)]
        return pltpu.make_async_copy(src, self.left.at[c - self.ends], self.l_s.at[c - self.ends])

    def result(self, c):
        src = self.ring.at[lax.rem(c, self.slots), self.rows(self.z)]
        return pltpu.make_async_copy(src, self.out.at[c], self.o_s.at[0])

    def finish(self, c):
        for h in range(self.zs):

            @pl.when(h < self.z)
            def _():
                self.dn(c, h).wait_send()

            @pl.when(h > self.z)
            def _():
                self.up(c, h).wait_send()

        self.result(c).start()


def mlp_kernel(zs, nc, n1, n2, fc, skip, *refs):
    refs = list(refs)

    def take(count):
        out = refs[:count]
        del refs[:count]
        return out

    if n1:
        mats, full_one = take(3), take(1)[0]
        mine = None
    else:
        (mine,) = take(1)
    h2, dy, dh2_out, y_out, g_out, full, r_sib, r_dn, r_up = take(9)
    left = take(1)[0] if n2 < nc else None
    acc_y, acc_d, h2t, dyt, wbuf, hid_s, dgu_s, ring, to_sib, tmp_s, tmp_d, tmp_u = take(12)
    d_src, d_own, d_one, d_two = take(4)
    w_sem, x_s, x_r, k_s, sq_sem, st_sem = take(6)
    sems = refs
    b, z, x = lax.axis_index("batch"), lax.axis_index("z"), lax.axis_index("x")
    greet(z, zs)
    rest = nc - n1
    lag = 0 if n1 else zs
    ahead = n1 - zs + 1 if n1 else 0
    gather = Gather(zs, mine, full, sems[:6])
    reduce = Reduce(
        zs, n2, ring, to_sib, r_sib, r_dn, r_up, (tmp_s, tmp_d, tmp_u), g_out, left, sems[6:]
    )
    slots = ring.shape[0]
    half = ring.shape[1]
    toks = h2.shape[0]
    block = toks // 2
    part = toks // 4
    square = Square(d_src, d_own, d_one, d_two, Pool(sq_sem))

    if n1:
        trade = Exchange(
            mats, full, n1, zs, skip, [lambda i, r=r: r.at[i] for r in (x_s, x_r, k_s)]
        )
        stage = [ring.at[ring.shape[0] - 1], ring.at[ring.shape[0] - 2]]
        for c in range(rest):
            for side in range(2):
                trade.fetch(c, side, stage[side], st_sem.at[2 * c + side])

        def slices(c):
            rows = pl.ds(c * trade.rows, trade.rows)
            dst = full.at[c, trade.at]
            return (
                pltpu.make_async_copy(stage[0].at[rows], dst, k_s.at[c]),
                remote(stage[1].at[rows], dst, x_s.at[c], x_r.at[c], {"x": 1 - x}),
            )

        for c in range(rest):
            for side in range(2):
                rows = stage[side].at[pl.ds(c * trade.rows, trade.rows)]
                pltpu.make_async_copy(rows, rows, st_sem.at[2 * c + side]).wait()
                slices(c)[side].start()

    def weights(c):
        return pltpu.make_async_copy(full.at[c - n1], wbuf, w_sem.at[0])

    def weights_one(c):
        return pltpu.make_async_copy(full_one.at[c], wbuf, w_sem.at[0])

    if n1:
        weights_one(0).start()
    acc_y[...] = jnp.zeros_like(acc_y)
    acc_d[...] = jnp.zeros_like(acc_d)
    for m in range(4):
        at = slice(m * block // 2, (m + 1) * block // 2)
        h2t[:, at] = h2[at].T
        dyt[:, at] = dy[at].T

    def compute(c):
        col = lax.broadcasted_iota(jnp.int32, (1, fc), 1) + c * fc
        live = jnp.where((col >= skip) | (x == 0), 1.0, 0.0).astype(F32)
        for m in range(2):
            at = slice(m * block, (m + 1) * block)
            gate_up = dot(h2[at], wbuf[:, : 2 * fc])
            d_hidden = dot(dy[at], wbuf[:, 2 * fc :]) * live
            gate, up = gate_up[:, :fc], gate_up[:, fc:]
            sig = 1.0 / (1.0 + jnp.exp(-gate))
            silu = gate * sig
            hid_s[at] = (silu * up * live).astype(BF)
            dgu_s[at, :fc] = (d_hidden * up * sig * (1.0 + gate * (1.0 - sig))).astype(BF)
            dgu_s[at, fc:] = (d_hidden * silu).astype(BF)
            acc_y[at] += dot_nt(hid_s[at], wbuf[:, 2 * fc :])
            acc_d[at] += dot_nt(dgu_s[at], wbuf[:, : 2 * fc])

        @pl.when(c == nc - 1)
        def _():
            for i in range(4):
                d_src[i] = acc_d[i * part : (i + 1) * part].astype(BF)
            square.start()

        @pl.when(c > 0)
        def _():
            reduce.sib(c - 1).wait_send()

        theirs = pl.ds(pl.multiple_of((1 - b) * half, half), half)
        own = pl.ds(pl.multiple_of(b * half, half), half)
        to_sib[:, : 2 * fc] = dot(h2t[theirs], dgu_s[...]).astype(BF)
        to_sib[:, 2 * fc :] = dot(dyt[theirs], hid_s[...]).astype(BF)
        reduce.sib(c).start()
        slot = lax.rem(c, slots)
        ring[slot, :, : 2 * fc] = dot(h2t[own], dgu_s[...]).astype(BF)
        ring[slot, :, 2 * fc :] = dot(dyt[own], hid_s[...]).astype(BF)

    def begin(i):
        @pl.when(in_range(i, rest))
        def _():
            if n1:
                trade.arrived(i, i)
            gather.start(i)

    def tick(t, carry):
        if n1:
            @pl.when(t == slots - 3)
            def _():
                for c in range(rest):
                    trade.sent(c, c)

        g = t + ahead
        begin(g)
        for k in range(1, zs):

            @pl.when(in_range(g - k, rest))
            def _():
                gather.hop(g - k, k)

        @pl.when(in_range(g - zs, rest))
        def _():
            gather.finish(g - zs)

        c = t - lag
        c_sib = c - 1
        c_dn = c_sib - 2 * (zs - 1 - z)
        c_up = c_sib - 2 * z
        c_end = c_sib - 2 * zs + 1

        @pl.when(in_range(c - n1, rest))
        def _():
            weights(c).start()

        if n1:

            @pl.when((c > 0) & (c < n1))
            def _():
                weights_one(c).start()

        reduce.arrive(c_sib, c_dn, c_up, nc)
        reduce.pass_on(c_sib, c_dn, c_up, nc)

        @pl.when(in_range(c_end, n2))
        def _():
            reduce.finish(c_end)
            reduce.result(c_end).wait()

        @pl.when(in_range(c, nc))
        def _():
            weights(n1).wait()
            compute(c)

        return carry

    for i in range(ahead):
        begin(i)
    lax.fori_loop(0, nc + lag, tick, 0)

    lax.fori_loop(nc + lag, nc + lag + 1, tick, 0)
    square.turn()
    for copy in square.first():
        copy.wait_send()
    for i in range(4):
        d_src[i] = acc_y[i * part : (i + 1) * part].astype(BF)
    y_copy = pltpu.make_async_copy(d_src, y_out, w_sem.at[0])
    y_copy.start()
    lax.fori_loop(nc + lag + 1, max(nc + 1, n2 + 2 * zs) + lag, tick, 0)
    dh2_out[...] = square.result()
    for copy in square.second():
        copy.wait_send()
    y_copy.wait()
    reduce.sib(nc - 1).wait_send()
    for c in range(n2, nc):
        reduce.leave(c).wait()

    def drain(c, carry):
        gather.drain(c)
        return carry

    lax.fori_loop(0, rest, drain, 0)


def mlp_call(zs, nc, n1, n2, fc, skip, weights, h2, dy):
    toks, width = h2.shape
    half = width // 2
    slots = min(2 * zs, nc)
    rest = nc - n1
    dma = pltpu.SemaphoreType.DMA
    vm = pltpu.VMEM
    shape = jax.ShapeDtypeStruct
    any_spec = pl.BlockSpec(memory_space=pl.ANY)
    out = [
        shape((toks // 4, width), F32),
        shape((4, toks // 4, width), BF),
        shape((n2, half // zs, 3 * fc), BF),
        shape((rest, width, 3 * fc), BF),
        shape((nc, half, 3 * fc), BF),
        shape((n2, half, 3 * fc), BF),
        shape((n2, half, 3 * fc), BF),
    ]
    if n2 < nc:
        out.append(shape((nc - n2, half, 3 * fc), BF))
    result = pl.pallas_call(
        functools.partial(mlp_kernel, zs, nc, n1, n2, fc, skip),
        out_shape=out,
        in_specs=[any_spec] * len(weights) + [VMEM, VMEM],
        out_specs=[VMEM] + [any_spec] * (len(out) - 1),
        scratch_shapes=[
            vm((toks, width), F32),
            vm((toks, width), F32),
            vm((width, toks), BF),
            vm((width, toks), BF),
            vm((width, 3 * fc), BF),
            vm((toks, fc), BF),
            vm((toks, 2 * fc), BF),
            vm((slots, half, 3 * fc), BF),
            vm((half, 3 * fc), BF),
            vm((half, 3 * fc), BF),
            vm((half, 3 * fc), BF),
            vm((half, 3 * fc), BF),
            vm((4, toks // 4, width), BF),
            vm((4, toks // 4, half), BF),
            vm((4, toks // 4, half), BF),
            vm((2, toks // 4, half), BF),
            dma((1,)),
        ]
        + [dma((rest,))] * 3
        + [dma((13,)), dma((2 * rest,)), dma((rest,))]
        + [dma((rest, zs))] * 5
        + [dma((nc,))] * 2
        + [dma((nc, zs))] * 4
        + [dma((1 + 2 * zs,)), dma((1,)), dma((nc,))],
        compiler_params=pltpu.CompilerParams(
            collective_id=0, has_side_effects=True, vmem_limit_bytes=62 * 2**20
        ),
        cost_estimate=pl.CostEstimate(
            flops=18 * toks * width * fc * nc, bytes_accessed=80 * 2**20, transcendentals=0
        ),
    )(*weights, h2, dy)
    return list(result[:3]) + list(result[7:])


def final_kernel(skip, *refs):
    refs = list(refs)
    inputs = refs[:8]
    d_hidden, g_query, g_key, g_value, g_out, g_gate, g_up, g_down, output = refs[8:17]
    bufs, sem = refs[17:24] + [output], refs[24]
    x = lax.axis_index("x")
    copies = [
        pltpu.make_async_copy(src, dst, sem.at[i])
        for i, (src, dst) in enumerate(zip(inputs, bufs))
    ]
    for copy in copies:
        copy.start()
    near, left, far, gh, s_q, s_kv, s_wo, _ = bufs
    n2, nl = near.shape[0], left.shape[0]
    half = gh.shape[1]
    fc = far.shape[2] // 3
    split = (n2 + nl) * fc
    for i in (0, 2, 1):
        copies[i].wait()
    for c in range(n2 + nl):
        own = (near[c, x] if c < n2 else left[c - n2]).astype(F32)
        other = far[c].astype(F32)
        low = jnp.where(x == 0, own, other)
        high = jnp.where(x == 0, other, own)
        for w, out in enumerate((g_gate, g_up, g_down)):
            b = high[:, w * fc : (w + 1) * fc]
            first = split - skip + c * fc
            if c == 0:
                b = b[:, skip:]
                first = split
            out[:, c * fc : (c + 1) * fc] = low[:, w * fc : (w + 1) * fc]
            out[:, first : first + b.shape[1]] = b
    for i in (3, 4, 5, 6):
        copies[i].wait()
    for i in range(2):
        d_hidden[i * half : (i + 1) * half] = gh[i].astype(F32)
    g_query[...] = s_q[...].astype(F32)
    g_key[...] = s_kv[:, :HEAD_SIZE].astype(F32)
    g_value[...] = s_kv[:, HEAD_SIZE:].astype(F32)
    g_out[...] = s_wo[...].astype(F32)
    copies[7].wait()


def final_call(skip, ff, inputs):
    rows, three = inputs[2].shape[1:]
    _, half, width = inputs[3].shape
    q_cols = inputs[4].shape[1]
    shape = jax.ShapeDtypeStruct
    any_spec = pl.BlockSpec(memory_space=pl.ANY)
    out = [
        shape((2 * half, width), F32),
        shape((rows, q_cols), F32),
        shape((rows, HEAD_SIZE), F32),
        shape((rows, HEAD_SIZE), F32),
        shape((rows, q_cols), F32),
        shape((rows, ff), F32),
        shape((rows, ff), F32),
        shape((rows, ff), F32),
        shape(inputs[7].shape, BF),
    ]
    return pl.pallas_call(
        functools.partial(final_kernel, skip),
        out_shape=out,
        in_specs=[any_spec] * len(inputs),
        out_specs=[VMEM] * 9,
        scratch_shapes=[pltpu.VMEM(v.shape, BF) for v in inputs[:7]]
        + [pltpu.SemaphoreType.DMA((8,))],
        compiler_params=pltpu.CompilerParams(vmem_limit_bytes=60 * 2**20),
    )(*inputs)


def on_device(
    hidden,
    lengths,
    norm_attn,
    w_query,
    key_weight_matrix,
    value_weight_matrix,
    b_query,
    key_bias_rows,
    value_bias_rows,
    w_out,
    norm_mlp,
    w_gate,
    w_up,
    w_down,
    cotangent,
):
    homes = lax.axis_size("batch") * lax.axis_size("z") * lax.axis_size("x")
    shards = lax.axis_size("z") * lax.axis_size("x")
    z_i, x_i = lax.axis_index("z"), lax.axis_index("x")
    me = z_i * lax.axis_size("x") + x_i
    tok = hidden.shape[1]
    width = hidden.shape[2]
    half = tok // 2
    doc_lengths = lengths[0]
    heads = b_query.shape[0]
    heads_all = heads + 2
    q_cols = heads * HEAD_SIZE
    rows = norm_attn.shape[0]
    ff = w_gate.shape[1]
    ffh = -(-ff // 512) * 256
    fc = FC
    nc = ffh // fc

    home = (lax.axis_index("batch") * lax.axis_size("z") + z_i) * 2 + x_i
    per_home = HEAD_SIZE // homes

    def spot(value, count):
        out = jnp.zeros((value.shape[0], homes, count), BF)
        return lax.dynamic_update_slice(out, value[:, None, :], (0, home, 0)).reshape(-1)

    biases = jnp.concatenate([b_query, key_bias_rows, value_bias_rows], axis=0)
    small = jnp.concatenate(
        [spot(biases, per_home), spot(norm_attn[None], rows), spot(norm_mlp[None], rows)]
    ).reshape(16, -1)
    w_qkv = jnp.concatenate([w_query, key_weight_matrix, value_weight_matrix], axis=1)

    zs = lax.axis_size("z")
    n1, n2 = (zs, nc - zs + 1) if rows % 16 == 0 and 2 * zs < nc else (0, nc)
    three = (w_gate, w_up, w_down.T)
    skip = 2 * ffh - ff

    stored = me * tok + jnp.arange(tok, dtype=jnp.int32)
    q_rows = row_positions(stored, shards, half)
    doc_start = doc_starts_of(q_rows, doc_lengths)
    cosine_table, sine_table = rotary(q_rows - doc_start, HEAD_SIZE)
    cos2 = jnp.concatenate([cosine_table, cosine_table], axis=1)
    sin2 = jnp.concatenate([-sine_table, sine_table], axis=1)
    start_row = doc_start[None, :]

    x_in = hidden[0]
    (
        h_first,
        q_mat,
        out_low,
        lse,
        mid,
        vec,
        wqkv,
        wo_t,
        kv_all,
        h2,
        dy,
        *full_one,
    ) = forward_call(
        zs,
        heads,
        n1,
        skip,
        fc,
        x_in,
        w_qkv,
        w_out.T,
        small,
        cos2,
        sin2,
        start_row,
        cotangent[0].reshape(2, half, width),
        three if n1 else (),
    )
    h2 = h2.reshape(4 * half, width)
    dy = dy.reshape(4 * half, width)
    if n1:
        mlp_w = (*three, *full_one)
    else:

        def stacked(x_at):
            halves = [
                lax.dynamic_slice_in_dim(mat, x_at * (ff - ffh), ffh, axis=1).reshape(rows, nc, fc)
                for mat in three
            ]
            return jnp.transpose(jnp.concatenate(halves, axis=2), (1, 0, 2))

        keep = stacked(x_i)
        other = lax.ppermute(stacked(1 - x_i), "x", [(0, 1), (1, 0)])
        low = jnp.where(x_i == 0, keep, other)
        high = jnp.where(x_i == 0, other, keep)
        mlp_w = (jnp.concatenate([low, high], axis=1),)
    dh2, y_sum, mlp_g, *left = mlp_call(zs, nc, n1, n2, fc, skip, mlp_w, h2, dy)
    mlp_g = mlp_g.reshape(n2, 2, rows, 3 * fc)
    left = [v.reshape(nc - n2, zs, 2 * rows, 3 * fc) for v in left]

    output, d_hidden, s_q, s_kv, s_wo, g_vec, other, *left_own = backward_call(
        zs,
        heads,
        left,
        (y_sum, mlp_g),
        (
            dh2,
            mid,
            vec,
            x_in,
            cotangent[0],
            h_first,
            q_mat,
            out_low,
            lse[:, None],
            kv_all,
            wqkv,
            wo_t,
            cos2,
            sin2,
            start_row.reshape(2, 1, half),
        ),
    )
    g_vec = g_vec.reshape(-1)
    g_bias = lax.dynamic_slice_in_dim(
        g_vec[: heads_all * HEAD_SIZE].reshape(heads_all, HEAD_SIZE), home * per_home, per_home, 1
    )
    g_norms = g_vec[heads_all * HEAD_SIZE :].reshape(2, width)
    g_norms = lax.dynamic_slice_in_dim(g_norms, home * rows, rows, 1)

    if n1:
        grads = final_call(skip, ff, (mlp_g, *left_own, other, d_hidden, s_q, s_kv, s_wo, output))
    else:
        keep = lax.dynamic_index_in_dim(mlp_g, x_i, 1, False)
        low = jnp.where(x_i == 0, keep, other)
        high = jnp.where(x_i == 0, other, keep)

        def whole(k):
            def cols(value):
                piece = value[:, :, k * fc : (k + 1) * fc]
                return jnp.transpose(piece, (1, 0, 2)).reshape(rows, ffh)

            return jnp.concatenate([cols(low), cols(high)[:, skip:]], axis=1).astype(F32)

        grads = (
            d_hidden.astype(F32).reshape(tok, width),
            s_q.astype(F32),
            s_kv[:, :HEAD_SIZE].astype(F32),
            s_kv[:, HEAD_SIZE:].astype(F32),
            s_wo.astype(F32),
            whole(0),
            whole(1),
            whole(2),
            output,
        )
    d_hidden, g_query, g_key, g_value, g_out, g_gate, g_up, g_down, output = grads
    return (
        output.reshape(1, tok, width),
        d_hidden[None],
        g_norms[0],
        g_query,
        g_key,
        g_value,
        g_bias[:heads],
        g_bias[heads : heads + 1],
        g_bias[heads + 1 :],
        g_out.T,
        g_norms[1],
        g_gate,
        g_up,
        g_down.T,
    )


def solution(mesh):
    seq = mesh.shape["seq"]
    fine = Mesh(
        mesh.devices.reshape(mesh.shape["batch"], seq // 2, 2, mesh.shape["tensor"]),
        ("batch", "z", "x", "tensor"),
    )
    toks = P("batch", ("z", "x"), None)
    home = ("batch", "z", "x")
    down = P(home, "tensor")
    across = P("tensor", home)
    return jax.shard_map(
        on_device,
        mesh=fine,
        in_specs=(
            toks,
            P("batch", None),
            P(home),
            down,
            down,
            down,
            across,
            across,
            across,
            across,
            P(home),
            down,
            down,
            across,
            toks,
        ),
        out_specs=(
            toks,
            toks,
            P(home),
            down,
            down,
            down,
            across,
            across,
            across,
            across,
            P(home),
            down,
            down,
            across,
        ),
        check_vma=False,
    )
```

time: 2190 us -> 482 us (0.22)
  the two profiles are of different devices: /device:TPU:8 before, /device:TPU:24 now
where the time goes in v1:
time: 482 us; the launch traced here: 474 us
  Pallas kernels  463 us (96%)
  other arithmetic  5.12 us (1%)
    pallas_call x1, Pallas kernels, mlp_call(): pl.pallas_call(functools.partial(mlp_kernel, zs, nc, n1, n2, fc, skip), o...  202 us
    pallas_call x1, Pallas kernels, backward_call(): pl.pallas_call(functools.partial(backward_kernel, zs, heads, nl, HEAD_SIZ...  129 us
    pallas_call x1, Pallas kernels, forward_call(): pl.pallas_call(functools.partial(forward_kernel, zs, heads, n1, skip, HEA...  126 us

profile of v1, /device:TPU:24, one launch (start us, length us, event | category | flops | bytes accessed | tf_op | source)
XLA Modules:
  0.0 473.6 jit_solution(6875294904584109536)
XLA Ops:
  0.6 0.0 copy-start
  0.7 0.0 copy-start.3
  0.7 0.0 copy-start.2
  0.7 0.8 maximum_bitcast_fusion
  1.5 0.1 reshape.148
  1.6 0.7 dynamic_update_slice.10
  2.3 0.1 reshape.149
  2.4 0.7 dynamic_update_slice.11
  3.1 0.1 reshape.150
  3.2 0.6 reshape.151.small_in
  3.8 0.8 reduce-window.4
  4.7 0.7 fusion.8
  5.3 0.1 select_reduce_fusion
  5.4 0.0 copy-start.5
  5.5 1.0 fusion
  6.5 1.0 pad_maximum_fusion
  7.5 0.0 copy-done
  7.5 0.0 copy-done.3
  7.5 0.0 copy-done.2
  7.5 0.7 pad_maximum_fusion.2.wqkv_in
  8.2 0.0 copy-done.5
  8.2 125.6 %shard_map.254 = (bf16[512,1536]{1,0:T(8,128)(2,1)}, bf16[512,768]{1,0:T(8,128)(2,1)}, bf16[512,768]{1,0:T(8,128)(2,1)}, f32[2,1536]{1,0:T(2,128)}, f32[256,1536...) custom-call(bf16[512,1536]{1,0:T(8,128)(2,1)} %bitcast.42, ...), custom_call_target="tpu_custom_call" | custom-call | flops 4966055936 | bytes 33554432 | tf_op jit(solution)/shard_map/pallas_call | solution.py:599
  133.8 0.0 copy-start.4
  133.8 201.6 %shard_map.255 = (f32[256,1536]{1,0:T(8,128)}, bf16[4,256,1536]{2,1,0:T(8,128)(2,1)}, bf16[6,192,768]{2,1,0:T(8,128)(2,1)}, bf16[5,1536,768]{2,1,0:T(8,128)(2,1)...) custom-call(bf16[96,4480]{1,0:T(8,128)(2,1)} %refs_0_.3, ...), custom_call_target="tpu_custom_call" | custom-call | flops 65229815808 | bytes 83886080 | tf_op jit(solution)/shard_map/pallas_call | solution.py:1967
  335.4 0.0 copy-done.4
  335.4 0.6 broadcast_in_dim.36.refs_11_
  336.1 128.6 %shard_map.256 = (bf16[2,256,1536]{2,1,0:T(8,128)(2,1)}, bf16[2,256,1536]{2,1,0:T(8,128)(2,1)}, bf16[96,768]{1,0:T(8,128)(2,1)}, bf16[96,256]{1,0:T(8,128)(2,1)}...) custom-call(bf16[4,256,1536]{2,1,0:T(8,128)(2,1)} %get-tuple-element.5, ...), custom_call_target="tpu_custom_call" | custom-call | flops 9932111872 | bytes 33554432 | tf_op jit(solution)/shard_map/pallas_call | solution.py:1394
  464.7 0.0 copy-start.1
  464.7 7.2 %shard_map.257 = (f32[512,1536]{1,0:T(8,128)}, f32[96,768]{1,0:T(8,128)}, f32[96,128]{1,0:T(8,128)}, f32[96,128]{1,0:T(8,128)}, f32[96,768]{1,0:T(8,128)}, /*ind...) custom-call(bf16[6,2,96,768]{3,2,1,0:T(8,128)(2,1)} %bitcast.33, ...), custom_call_target="tpu_custom_call" | custom-call | tf_op jit(solution)/shard_map/pallas_call | solution.py:2067
  471.9 0.0 copy-done.1
  471.9 0.1 constant_dynamic-slice_fusion
  472.0 0.5 slice_bitcast_fusion
  472.5 0.1 constant_dynamic-slice_fusion.1
  472.6 0.0 copy-start.6
  472.6 0.5 fusion.9
  473.1 0.1 copy-done.6
  (13 shorter events, 0.2 us)
Async XLA Ops:
  0.6 6.8 %copy-start = (bf16[96,768]{1,0:T(8,128)(2,1)S(1)}, bf16[96,768]{1,0:T(8,128)(2,1)}, u32[]{:S(2)}) copy-start(bf16[96,768]{1,0:T(8,128)(2,1)} %param.18) | copy-start | bytes 442372
  0.7 6.8 %copy-start.3 = (bf16[96,128]{1,0:T(8,128)(2,1)S(1)}, bf16[96,128]{1,0:T(8,128)(2,1)}, u32[]{:S(2)}) copy-start(bf16[96,128]{1,0:T(8,128)(2,1)} %param.19) | copy-start | bytes 73732
  0.7 6.8 %copy-start.2 = (bf16[96,128]{1,0:T(8,128)(2,1)S(1)}, bf16[96,128]{1,0:T(8,128)(2,1)}, u32[]{:S(2)}) copy-start(bf16[96,128]{1,0:T(8,128)(2,1)} %param.20) | copy-start | bytes 73732
  5.4 2.8 copy-start.5
  133.8 201.6 %copy-start.4 = (f32[2,1536]{1,0:T(2,128)S(1)}, f32[2,1536]{1,0:T(2,128)}, u32[]{:S(2)}) copy-start(f32[2,1536]{1,0:T(2,128)} %get-tuple-element.59) | copy-start | bytes 36868
  464.7 7.2 %copy-start.1 = (f32[16,256]{1,0:T(8,128)S(1)}, f32[16,256]{1,0:T(8,128)}, u32[]{:S(2)}) copy-start(f32[16,256]{1,0:T(8,128)} %get-tuple-element.72) | copy-start | bytes 49156
  472.6 0.6 copy-start.6

commit v2 on v1

--- a/solution.py
+++ b/solution.py
@@ -219,7 +219,8 @@
     skip,
     scale,
     x_ref,
-    wqkv_in,
+    wkv_in,
+    wq_in,
     wo_in,
     small_in,
     cos_ref,
@@ -233,13 +234,13 @@
         mats = refs[:3]
         del refs[:3]
     h1_out, q_out, attn_out, lse_out, mid_out, vec_out = refs[:6]
-    wqkv_all, wo_all, kv_all, h2_all, dy_all = refs[6:11]
-    del refs[:11]
+    wkv_all, wq_all, wo_all, kv_all, h2_all, dy_all = refs[6:12]
+    del refs[:12]
     if n1:
         full = refs.pop(0)
-    small_buf, wqkv_buf, wo_buf, kv_buf, q_t, acc_ref, max_ref, sum_ref = refs[:8]
-    att_send, att_recv, h2_half, xn_ref, sem_ref = refs[8:13]
-    g_sems = refs[13:]
+    small_buf, wkv_buf, wq_buf, wo_buf, kv_buf, q_t, acc_ref, max_ref, sum_ref = refs[:9]
+    att_send, att_recv, h2_half, xn_ref, sem_ref = refs[9:14]
+    g_sems = refs[14:]
     b, z, x, t = (lax.axis_index(a) for a in ("batch", "z", "x", "tensor"))
     shards = 2 * zs
     me = 2 * z + x
@@ -250,11 +251,12 @@
     greet(z, zs)
 
     small = Spread(zs, small_in, small_buf, pool)
-    wqkv = Spread(zs, wqkv_in, wqkv_buf, pool)
+    wkv = Spread(zs, wkv_in, wkv_buf, pool)
+    wq = Spread(zs, wq_in, wq_buf, pool)
     wo = Spread(zs, wo_in, wo_buf, pool)
     small.start()
-    wqkv.start()
-    wo.start()
+    wkv.start()
+    wq.start()
 
     runs = thirds(zs)
     if n1:
@@ -293,18 +295,19 @@
     dy_piece = dy_all.at[2 * (1 - x) + t, pl.ds(0, quarter)]
     dy_across = remote(dy_piece, dy_piece, dyy_s(), dyy_r(), {"tensor": 1 - t})
 
-    ship(0, 2)
     for m in range(2):
         at = slice(m * half, (m + 1) * half)
         xv = x_ref[at].astype(F32)
         xn_ref[at] = xv * norm_factor(xv)
     for k in range(1, zs):
         small.hop(k)
-        wqkv.hop(k)
+        wkv.hop(k)
+        if k == 1:
+            ship(0, 1)
+    for k in runs[0]:
+        wq.hop(k)
+    wo.start()
     prefetch(0)
-    ship(2, 3)
-    for k in runs[0]:
-        wo.hop(k)
     small.cross()
     small.finish()
     vec = jnp.sum(small_buf[...].astype(F32), axis=0)
@@ -316,22 +319,20 @@
         at = slice(m * half, (m + 1) * half)
         h1_out[at] = (xn_ref[at] * gain_attn).astype(BF)
 
-    wqkv.cross()
-    prefetch(1)
-    wqkv.finish()
-    wqkv_m = merge_rows(wqkv_buf[...])
+    def turned(value, at):
+        return value * cos_ref[at] + pltpu.roll(value, HEAD_SIZE // 2, 1) * sin_ref[at]
+
+    wkv.cross()
+    ship(1, 2)
+    wkv.finish()
+    for k in runs[1]:
+        wq.hop(k)
+    wkv_m = merge_rows(wkv_buf[...])
     for m in range(2):
         at = slice(m * half, (m + 1) * half)
-        lin = dot(h1_out[at], wqkv_m) + bias
-        cos, sin = cos_ref[at], sin_ref[at]
-        for h in range(heads + 1):
-            v = lin[:, h * HEAD_SIZE : (h + 1) * HEAD_SIZE]
-            v = (v * cos + pltpu.roll(v, HEAD_SIZE // 2, 1) * sin).astype(BF)
-            if h < heads:
-                q_out[at, h * HEAD_SIZE : (h + 1) * HEAD_SIZE] = v
-            else:
-                kv_buf[me + m, :, :HEAD_SIZE] = v
-        kv_buf[me + m, :, HEAD_SIZE:] = lin[:, (heads + 1) * HEAD_SIZE :].astype(BF)
+        lin = dot(h1_out[at], wkv_m) + bias[:, q_cols:]
+        kv_buf[me + m, :, :HEAD_SIZE] = turned(lin[:, :HEAD_SIZE], at).astype(BF)
+        kv_buf[me + m, :, HEAD_SIZE:] = lin[:, HEAD_SIZE:].astype(BF)
 
     ku_s, kd_s, k0_r, k1_r, x0_s, x1_s, x0_r, x1_r = (pool.take(zs) for _ in range(8))
 
@@ -348,6 +349,29 @@
         send, recv = (x0_s, x0_r) if sub == 0 else (x1_s, x1_r)
         return remote(piece, piece, send(s), recv(s), {"x": 1 - x})
 
+    def kv_hop(k):
+        low, high = z - k, z + k
+
+        @pl.when(low >= 0)
+        def _():
+            kv_up(low).wait_recv()
+
+            @pl.when(z < zs - 1)
+            def _():
+                kv_up(low).start()
+
+            kv_side(low, 0, x).start()
+
+        @pl.when(high < zs)
+        def _():
+            kv_dn(high).wait_recv()
+
+            @pl.when(z > 0)
+            def _():
+                kv_dn(high).start()
+
+            kv_side(high, 1, x).start()
+
     @pl.when(z < zs - 1)
     def _():
         kv_up(z).start()
@@ -364,8 +388,27 @@
     def _():
         kv_side(z, 1, x).start()
 
+    for k in runs[2]:
+        wq.hop(k)
+    for k in runs[0]:
+        wo.hop(k)
+    for k in runs[0]:
+        kv_hop(k)
+    wq.cross()
+    for k in runs[1]:
+        kv_hop(k)
     for k in runs[1]:
         wo.hop(k)
+    ship(2, 3)
+    prefetch(1)
+    wq.finish()
+    wq_m = merge_rows(wq_buf[...])
+    for m in range(2):
+        at = slice(m * half, (m + 1) * half)
+        lin = dot(h1_out[at], wq_m) + bias[:, :q_cols]
+        for h in range(heads):
+            cols = slice(h * HEAD_SIZE, (h + 1) * HEAD_SIZE)
+            q_out[at, cols] = turned(lin[:, cols], at).astype(BF)
     for sub in range(2):
         q_t[sub] = stack_heads(q_out, sub, half, heads).T
     acc_ref[...] = jnp.zeros_like(acc_ref)
@@ -392,30 +435,6 @@
 
         @pl.when((low >= 0) & (k < zs))
         def _():
-            @pl.when(k > 0)
-            def _():
-                kv_up(low).wait_recv()
-
-                @pl.when(z < zs - 1)
-                def _():
-                    kv_up(low).start()
-
-                kv_side(low, 0, x).start()
-
-        @pl.when((high < zs) & (k < zs))
-        def _():
-            @pl.when(k > 0)
-            def _():
-                kv_dn(high).wait_recv()
-
-                @pl.when(z > 0)
-                def _():
-                    kv_dn(high).start()
-
-                kv_side(high, 1, x).start()
-
-        @pl.when((low >= 0) & (k < zs))
-        def _():
             fold(0, 2 * low + x)
 
         @pl.when((high < zs) & (k < zs))
@@ -434,6 +453,11 @@
             kv_side(far_high, 1, 1 - x).wait_recv()
             fold(1, 2 * far_high + 1 - x)
 
+        @pl.when(k == 0)
+        def _():
+            for hop in runs[2]:
+                kv_hop(hop)
+
         @pl.when(k == 1)
         def _():
             for hop in runs[2]:
@@ -441,15 +465,17 @@
 
         @pl.when(k == 2)
         def _():
+            dy_side(1).start()
+
+        @pl.when(k == zs - 1)
+        def _():
             prefetch(2)
 
-        @pl.when(k == zs - 1)
-        def _():
-            ship(3, n1)
-
         return carry
 
     lax.fori_loop(0, zs + 1, attend, 0)
+    dy_side(0).start()
+    ship(3, n1)
     wo.cross()
     for sub in range(2):
         lse_out[sub : sub + 1, :] = max_ref[sub] + jnp.log(sum_ref[sub])
@@ -459,8 +485,6 @@
                 out_t[:, h * half : (h + 1) * half].T.astype(BF)
             )
 
-    dy_side(1).start()
-    dy_side(0).start()
     wo.finish()
     att_s, att_r = pool.take(2), pool.take(2)
     h_l, hx_s, hx_r, hy_s, hy_r = (pool.take(2) for _ in range(5))
@@ -501,28 +525,28 @@
     from_across = h2_all.at[2 * x + 1 - t, rows(1)]
     relay_across = remote(from_side, from_side, hyy_s(), hyy_r(), {"tensor": 1 - t})
     relay_side = remote(from_across, from_across, hxx_s(), hxx_r(), {"x": 1 - x})
+    dy_side(2).start()
     h_copies(0)[1].wait_recv()
     relay_across.start()
+    prefetch(4)
+    h_copies(1)[2].wait_recv()
+    relay_side.start()
     dy_side(0).wait_recv()
     dy_across.start()
-    prefetch(4)
-    dy_side(2).start()
-    h_copies(1)[2].wait_recv()
-    relay_side.start()
     for tick in range(5, n1 + 3):
         prefetch(tick)
 
-    save = pool.take(3)
+    save = pool.take(4)
     saves = [
         pltpu.make_async_copy(src, dst, save(i))
         for i, (src, dst) in enumerate(
-            ((wqkv_buf, wqkv_all), (wo_buf, wo_all), (kv_buf, kv_all))
+            ((wkv_buf, wkv_all), (wq_buf, wq_all), (wo_buf, wo_all), (kv_buf, kv_all))
         )
     ]
     for copy in saves:
         copy.start()
 
-    for item in (small, wqkv, wo):
+    for item in (small, wkv, wq, wo):
         item.drain()
 
     def kv_drain(s, carry):
@@ -570,13 +594,12 @@
 
 
 def forward_call(
-    zs, heads, n1, skip, fc, x_in, wqkv_in, wo_in, small_in, cos, sin, start, dy_in, first
+    zs, heads, n1, skip, fc, x_in, wkv_in, wq_in, wo_in, small_in, cos, sin, start, dy_in, first
 ):
     tok, width = x_in.shape
     half = tok // 2
     homes = 4 * zs
-    rows, qkv_cols = wqkv_in.shape
-    q_cols = heads * HEAD_SIZE
+    rows, q_cols = wq_in.shape
     shape = jax.ShapeDtypeStruct
     any_spec = pl.BlockSpec(memory_space=pl.ANY)
     out = [
@@ -586,24 +609,26 @@
         shape((2, heads * half), F32),
         shape((half, width), F32),
         shape(small_in.shape, F32),
-        shape((homes, rows, qkv_cols), BF),
+        shape((homes, rows, 2 * HEAD_SIZE), BF),
+        shape((homes, rows, q_cols), BF),
         shape((homes, rows, q_cols), BF),
         shape((2 * zs + 1, half, 2 * HEAD_SIZE), BF),
         shape((4, half, width), BF),
         shape((4, half, width), BF),
     ]
-    sems = [pltpu.SemaphoreType.DMA((3 * (9 * zs + 1) + 8 * zs + 3 * n1 + 36,))]
+    sems = [pltpu.SemaphoreType.DMA((4 * (9 * zs + 1) + 8 * zs + 3 * n1 + 40,))]
     if n1:
         out.append(shape((n1, width, 3 * fc), BF))
         sems += [pltpu.SemaphoreType.DMA((n1, zs))] * 5
     return pl.pallas_call(
         functools.partial(forward_kernel, zs, heads, n1, skip, HEAD_SIZE ** (-0.5)),
         out_shape=out,
-        in_specs=[VMEM] + [any_spec] * 3 + [VMEM] * (4 + len(first)),
+        in_specs=[VMEM] + [any_spec] * 4 + [VMEM] * (4 + len(first)),
         out_specs=[VMEM] * 6 + [any_spec] * (len(out) - 6),
         scratch_shapes=[
             pltpu.VMEM((homes,) + small_in.shape, BF),
-            pltpu.VMEM((homes, rows, qkv_cols), BF),
+            pltpu.VMEM((homes, rows, 2 * HEAD_SIZE), BF),
+            pltpu.VMEM((homes, rows, q_cols), BF),
             pltpu.VMEM((homes, rows, q_cols), BF),
             pltpu.VMEM((2 * zs + 1, half, 2 * HEAD_SIZE), BF),
             pltpu.VMEM((2, HEAD_SIZE, heads * half), BF),
@@ -620,11 +645,11 @@
             collective_id=1, has_side_effects=True, vmem_limit_bytes=60 * 2**20
         ),
         cost_estimate=pl.CostEstimate(
-            flops=2 * tok * width * (qkv_cols + q_cols) + 2**31,
+            flops=4 * tok * width * (q_cols + HEAD_SIZE) + 2**31,
             bytes_accessed=32 * 2**20,
             transcendentals=0,
         ),
-    )(x_in, wqkv_in, wo_in, small_in, cos, sin, start, dy_in, *first)
+    )(x_in, wkv_in, wq_in, wo_in, small_in, cos, sin, start, dy_in, *first)
 
 
 class Square:
@@ -705,7 +730,7 @@
         for copy in self.first():
             copy.wait_recv()
         for i in range(4):
-            self.own[i] = (self.own[i].astype(F32) + self.r_one[i].astype(F32)).astype(BF)
+            self.own[i] = self.own[i] + self.r_one[i]
         for copy in self.second():
             copy.start()
 
@@ -759,7 +784,7 @@
                 self.sib().start()
 
     def add(self, dst, src):
-        dst[...] = (dst[...].astype(F32) + src[...].astype(F32)).astype(BF)
+        dst[...] = dst[...] + src[...]
 
     def after_sib(self):
         self.sib().wait_recv()
@@ -879,8 +904,7 @@
 
     def plus(self, h, slot):
         for c in range(self.acc.shape[0]):
-            total = self.acc[c, h].astype(F32) + self.r_z[c, slot].astype(F32)
-            self.acc[c, h] = total.astype(BF)
+            self.acc[c, h] = self.acc[c, h] + self.r_z[c, slot]
 
     def step(self, k):
         def one(i, carry):
@@ -931,11 +955,11 @@
         del refs[:count]
         return out
 
-    y_in, g_mlp = take(2)
+    y_in, g_mlp, x_in, dy_in = take(4)
     if nl:
         (left_in,) = take(1)
-    dh2_ref, mid_ref, vec_ref, x_ref, dy_ref, h1_ref, q_ref, attn_ref, lse_ref, kv_ref = take(10)
-    wqkv_ref, wo_ref, cos_ref, sin_ref, start_ref = take(5)
+    dh2_ref, mid_ref, vec_ref, h1_ref, q_ref, attn_ref, lse_ref, kv_ref = take(8)
+    wkv_ref, wq_ref, wo_ref, cos_ref, sin_ref, start_ref = take(6)
     out_all, gh_all, g_q, g_kv, g_wo, g_vec, g_far = take(7)
     if nl:
         (left_out,) = take(1)
@@ -943,7 +967,7 @@
     q_s, do_s, q_t, do_t, delta_ref = take(5)
     dkv_ref, rx_ref, rz_ref, acc_ref, dqkv_ref, dh_send, dh_recv = take(7)
     bufs_q, bufs_kv, bufs_wo = take(5), take(5), take(5)
-    vec_own, vec_recv, vec_z, sem_ref = take(4)
+    vec_own, vec_recv, vec_z, x_ref, dy_ref, sem_ref = take(6)
     if nl:
         left_acc, left_z = take(2)
 
@@ -960,6 +984,12 @@
     col_kv = Collect(zs, *bufs_kv, g_kv, pool)
     col_wo = Collect(zs, *bufs_wo, g_wo, pool)
     runs = thirds(zs)
+    mine = pl.ds(pl.multiple_of(t * half, half), half)
+    fetch = pool.take(2)
+    x_load = pltpu.make_async_copy(x_in.at[mine], x_ref, fetch(0))
+    dy_load = pltpu.make_async_copy(dy_in.at[mine], dy_ref, fetch(1))
+    x_load.start()
+    dy_load.start()
     if nl:
         lines = [
             LineSum(zs, left_acc.at[pl.ds(c, 1)], left_z.at[pl.ds(c, 1)], pool) for c in range(nl)
@@ -982,8 +1012,8 @@
 
     mid = mid_ref[...]
     d_norm, g_norm_mlp = norm_backward(mid, norm_factor(mid), gain_mlp, dh2_ref[...])
-    mine = pl.ds(pl.multiple_of(t * half, half), half)
-    dmid_ref[...] = dy_ref[mine].astype(F32) + d_norm
+    dy_load.wait()
+    dmid_ref[...] = dy_ref[...].astype(F32) + d_norm
     dat_ref[t] = dmid_ref[...].astype(BF)
     dat_s, dat_r = pool.take(), pool.take()
 
@@ -1096,8 +1126,7 @@
         return dot(half_ref[at], attn_ref[...])
 
     def plus(slot, src):
-        total = dkv_ref[slot].astype(F32) + src[...].astype(F32)
-        dkv_ref[slot] = total.astype(BF)
+        dkv_ref[slot] = dkv_ref[slot] + src[...]
 
     def kv_begin():
         def one(i, carry):
@@ -1155,7 +1184,10 @@
     for i in range(2):
         half_ref[:, i * half : (i + 1) * half] = dat_ref[i].T
     col_wo.fill(wo_part)
-
+    for k in runs[0] + runs[1]:
+        kv_step(k)
+    line_tick(2)
+    col_wo.after_sib()
 
     def back(v, at):
         return v * cos_ref[at] - pltpu.roll(v, HEAD_SIZE // 2, 1) * sin_ref[at]
@@ -1166,8 +1198,7 @@
             v = acc_ref[sub, :, h * half : (h + 1) * half].T * scale
             dqkv_ref[at, h * HEAD_SIZE : (h + 1) * HEAD_SIZE] = back(v, at).astype(BF)
     half_ref[...] = h1_ref[...].T
-    col_wo.after_sib()
-    for k in runs[0]:
+    for k in runs[2]:
         kv_step(k)
 
     def part(first, last):
@@ -1178,12 +1209,6 @@
 
         return make
 
-    col_q.fill(part(0, q_cols))
-    for k in runs[1]:
-        kv_step(k)
-    line_tick(2)
-    for k in runs[2]:
-        kv_step(k)
     for sub in range(2):
         at = slice(sub * half, (sub + 1) * half)
         dk = dkv_ref[me + sub, :, :HEAD_SIZE].astype(F32)
@@ -1194,19 +1219,25 @@
     dh_copy = remote(dh_send, dh_recv, dh_s(), dh_r(), {"tensor": 1 - t})
     theirs = pl.ds(pl.multiple_of((1 - t) * half, half), half)
     own = pl.ds(pl.multiple_of(t * half, half), half)
-    dh_send[...] = dot_nt(dqkv_ref[theirs], merge_rows(wqkv_ref[...])).astype(BF)
+
+    def d_first(at):
+        q_part = dot_nt(dqkv_ref[at, :q_cols], merge_rows(wq_ref[...]))
+        return q_part + dot_nt(dqkv_ref[at, q_cols:], merge_rows(wkv_ref[...]))
+
+    dh_send[...] = d_first(theirs).astype(BF)
     dh_copy.start()
+    dh1 = d_first(own)
+    sq_y.turn()
     col_kv.fill(part(q_cols, q_cols + 2 * HEAD_SIZE))
-    dh1 = dot_nt(dqkv_ref[own], merge_rows(wqkv_ref[...]))
+    col_q.fill(part(0, q_cols))
+    line_tick(3)
     col_q.after_sib()
     col_kv.after_sib()
-    col_wo.after_side()
-    sq_y.turn()
-    line_tick(3)
 
     dh_copy.wait_recv()
     dh1 = dh1 + dh_recv[...].astype(F32)
-    xv = x_ref[mine].astype(F32)
+    x_load.wait()
+    xv = x_ref[...].astype(F32)
     d_norm, g_norm_attn = norm_backward(xv, norm_factor(xv), gain_attn, dh1)
 
     g_bias = jnp.sum(dqkv_ref[...].astype(F32), axis=0, keepdims=True)
@@ -1229,6 +1260,7 @@
         vec_own[...] = vec_own[...] + (other * norms if i == 0 else other)
 
     v_side(0).start()
+    line_tick(4)
     dat_copy(t).wait_send()
     dat_ref[t] = (dmid_ref[...] + d_norm).astype(BF)
     gh_s, gh_r, gh_l = (pool.take() for _ in range(3))
@@ -1236,9 +1268,9 @@
     gh_own = pltpu.make_async_copy(dat_ref.at[t], gh_all.at[t], gh_l())
     gh_copy.start()
     gh_own.start()
-    line_tick(4)
     v_add(0)
     v_side(1).start()
+    col_wo.after_side()
     far_s, far_r = pool.take(), pool.take()
     far_copy = remote(
         g_mlp.at[:, 1 - x],
@@ -1248,16 +1280,13 @@
         {"x": 1 - x},
     )
     far_copy.start()
-    col_kv.after_side()
+    line_tick(5)
     for k in runs[0]:
         col_wo.step(k)
-    if nl:
-        for tick in range(5, nl + 3):
-            line_tick(tick)
-    for k in runs[0]:
-        col_kv.step(k)
+    col_q.after_side()
     v_add(1)
     v_side(2).start()
+    col_kv.after_side()
     y_sum = sq_y.result()
     sq_y.drain()
     total = mid_ref[...] + y_sum
@@ -1271,9 +1300,13 @@
         locals_.append(pltpu.make_async_copy(y_own.at[i], dst, o_l(i)))
     for copy in sends + locals_:
         copy.start()
+    for tick in range(6, nl + 3):
+        line_tick(tick)
+    v_add(2)
+    for k in runs[0]:
+        col_q.step(k)
     for k in runs[1]:
         col_wo.step(k)
-    col_q.after_side()
     if nl:
         lf_s, lf_r, lf_l = (pool.take() for _ in range(3))
         rows = g_far.shape[1]
@@ -1291,9 +1324,8 @@
         left_own = pltpu.make_async_copy(left_rows(x), left_out, lf_l())
         left_far.start()
         left_own.start()
-    for k in runs[2]:
-        col_wo.step(k)
-    v_add(2)
+    for k in runs[0]:
+        col_kv.step(k)
 
     def v_copy(to):
         return remote(vec_own, vec_z.at[z], vz_s(to), vz_r(z), {"z": to})
@@ -1305,12 +1337,12 @@
             v_copy(to).start()
 
     for k in runs[1]:
+        col_q.step(k)
+    for k in runs[1]:
         col_kv.step(k)
-    for run in runs:
-        for k in run:
-            col_q.step(k)
-    for k in runs[2]:
-        col_kv.step(k)
+    for item in (col_wo, col_q, col_kv):
+        for k in runs[2]:
+            item.step(k)
     total = jnp.zeros(vec_ref.shape, F32)
     for frm in range(zs):
 
@@ -1368,11 +1400,11 @@
 
 def backward_call(zs, heads, left, big, small):
     mid, vec = small[1:3]
-    wqkv = small[10]
+    wq = small[9]
     half, width = mid.shape
     tok = 2 * half
-    _, rows, qkv_cols = wqkv.shape
-    q_cols = heads * HEAD_SIZE
+    _, rows, q_cols = wq.shape
+    qkv_cols = q_cols + 2 * HEAD_SIZE
     n2, _, _, three = big[1].shape
     nl = left[0].shape[0] if left else 0
     shape = jax.ShapeDtypeStruct
@@ -1403,7 +1435,7 @@
             shape((n2 + nl, rows, three), BF),
         ]
         + ([shape((nl, rows, three), BF)] if nl else []),
-        in_specs=[any_spec] * (2 + len(left)) + [VMEM] * len(small),
+        in_specs=[any_spec] * (4 + len(left)) + [VMEM] * len(small),
         out_specs=[any_spec] * 5 + [VMEM, any_spec] + [any_spec] * len(left),
         scratch_shapes=square
         + [
@@ -1430,6 +1462,8 @@
             vm(vec.shape, F32),
             vm((3,) + vec.shape, F32),
             vm((zs,) + vec.shape, F32),
+            vm((half, width), BF),
+            vm((half, width), BF),
             pltpu.SemaphoreType.DMA(((22 + 4 * nl) * zs + 90,)),
         ]
         + lines,
@@ -1681,8 +1715,7 @@
                 self.load_up(c_up, h).start()
 
     def add(self, slot, rows, tmp):
-        total = self.ring[slot, rows].astype(F32) + tmp[rows].astype(F32)
-        self.ring[slot, rows] = total.astype(BF)
+        self.ring[slot, rows] = self.ring[slot, rows] + tmp[rows]
 
     def pass_on(self, c_sib, c_dn, c_up, count):
         @pl.when(in_range(c_sib, count))
@@ -1782,7 +1815,6 @@
     slots = ring.shape[0]
     half = ring.shape[1]
     toks = h2.shape[0]
-    block = toks // 2
     part = toks // 4
     square = Square(d_src, d_own, d_one, d_two, Pool(sq_sem))
 
@@ -1820,25 +1852,29 @@
     acc_y[...] = jnp.zeros_like(acc_y)
     acc_d[...] = jnp.zeros_like(acc_d)
     for m in range(4):
-        at = slice(m * block // 2, (m + 1) * block // 2)
+        at = slice(m * part, (m + 1) * part)
         h2t[:, at] = h2[at].T
         dyt[:, at] = dy[at].T
 
+    nl = nc - n2
+
+    def keep_slot(c):
+        return jnp.maximum(c - n2, 0) if nl else 0
+
     def compute(c):
+        k = keep_slot(c)
         col = lax.broadcasted_iota(jnp.int32, (1, fc), 1) + c * fc
         live = jnp.where((col >= skip) | (x == 0), 1.0, 0.0).astype(F32)
-        for m in range(2):
-            at = slice(m * block, (m + 1) * block)
-            gate_up = dot(h2[at], wbuf[:, : 2 * fc])
-            d_hidden = dot(dy[at], wbuf[:, 2 * fc :]) * live
-            gate, up = gate_up[:, :fc], gate_up[:, fc:]
-            sig = 1.0 / (1.0 + jnp.exp(-gate))
-            silu = gate * sig
-            hid_s[at] = (silu * up * live).astype(BF)
-            dgu_s[at, :fc] = (d_hidden * up * sig * (1.0 + gate * (1.0 - sig))).astype(BF)
-            dgu_s[at, fc:] = (d_hidden * silu).astype(BF)
-            acc_y[at] += dot_nt(hid_s[at], wbuf[:, 2 * fc :])
-            acc_d[at] += dot_nt(dgu_s[at], wbuf[:, : 2 * fc])
+        gate_up = dot(h2[...], wbuf[:, : 2 * fc])
+        d_hidden = dot(dy[...], wbuf[:, 2 * fc :]) * live
+        gate, up = gate_up[:, :fc], gate_up[:, fc:]
+        sig = 1.0 / (1.0 + jnp.exp(-gate))
+        silu = gate * sig
+        hid_s[k] = (silu * up * live).astype(BF)
+        dgu_s[k, :, :fc] = (d_hidden * up * sig * (1.0 + gate * (1.0 - sig))).astype(BF)
+        dgu_s[k, :, fc:] = (d_hidden * silu).astype(BF)
+        acc_y[...] += dot_nt(hid_s[k], wbuf[:, 2 * fc :])
+        acc_d[...] += dot_nt(dgu_s[k], wbuf[:, : 2 * fc])
 
         @pl.when(c == nc - 1)
         def _():
@@ -1846,18 +1882,21 @@
                 d_src[i] = acc_d[i * part : (i + 1) * part].astype(BF)
             square.start()
 
+    def products(c):
+        k = keep_slot(c)
+
         @pl.when(c > 0)
         def _():
             reduce.sib(c - 1).wait_send()
 
         theirs = pl.ds(pl.multiple_of((1 - b) * half, half), half)
         own = pl.ds(pl.multiple_of(b * half, half), half)
-        to_sib[:, : 2 * fc] = dot(h2t[theirs], dgu_s[...]).astype(BF)
-        to_sib[:, 2 * fc :] = dot(dyt[theirs], hid_s[...]).astype(BF)
+        to_sib[:, : 2 * fc] = dot(h2t[theirs], dgu_s[k]).astype(BF)
+        to_sib[:, 2 * fc :] = dot(dyt[theirs], hid_s[k]).astype(BF)
         reduce.sib(c).start()
         slot = lax.rem(c, slots)
-        ring[slot, :, : 2 * fc] = dot(h2t[own], dgu_s[...]).astype(BF)
-        ring[slot, :, 2 * fc :] = dot(dyt[own], hid_s[...]).astype(BF)
+        ring[slot, :, : 2 * fc] = dot(h2t[own], dgu_s[k]).astype(BF)
+        ring[slot, :, 2 * fc :] = dot(dyt[own], hid_s[k]).astype(BF)
 
     def begin(i):
         @pl.when(in_range(i, rest))
@@ -1886,10 +1925,17 @@
             gather.finish(g - zs)
 
         c = t - lag
-        c_sib = c - 1
-        c_dn = c_sib - 2 * (zs - 1 - z)
-        c_up = c_sib - 2 * z
-        c_end = c_sib - 2 * zs + 1
+        c_dn = c - 1 - 2 * (zs - 1 - z)
+        c_up = c - 1 - 2 * z
+        c_end = c - 2 * zs
+
+        def product_at(step):
+            late = step - nl
+            return jnp.where(
+                in_range(step, n2), step, jnp.where((step >= nc) & (late < nc), late, -1)
+            )
+
+        c_sib = product_at(c - 1)
 
         @pl.when(in_range(c - n1, rest))
         def _():
@@ -1913,6 +1959,12 @@
         def _():
             weights(n1).wait()
             compute(c)
+
+        c_prod = product_at(c)
+
+        @pl.when(c_prod >= 0)
+        def _():
+            products(c_prod)
 
         return carry
 
@@ -1920,7 +1972,9 @@
         begin(i)
     lax.fori_loop(0, nc + lag, tick, 0)
 
-    lax.fori_loop(nc + lag, nc + lag + 1, tick, 0)
+    end = max(nc + nl + 1, n2 + 2 * zs) + lag
+    turn = min(nc + lag + 3, end)
+    lax.fori_loop(nc + lag, turn, tick, 0)
     square.turn()
     for copy in square.first():
         copy.wait_send()
@@ -1928,7 +1982,7 @@
         d_src[i] = acc_y[i * part : (i + 1) * part].astype(BF)
     y_copy = pltpu.make_async_copy(d_src, y_out, w_sem.at[0])
     y_copy.start()
-    lax.fori_loop(nc + lag + 1, max(nc + 1, n2 + 2 * zs) + lag, tick, 0)
+    lax.fori_loop(turn, end, tick, 0)
     dh2_out[...] = square.result()
     for copy in square.second():
         copy.wait_send()
@@ -1975,8 +2029,8 @@
             vm((width, toks), BF),
             vm((width, toks), BF),
             vm((width, 3 * fc), BF),
-            vm((toks, fc), BF),
-            vm((toks, 2 * fc), BF),
+            vm((max(nc - n2, 1), toks, fc), BF),
+            vm((max(nc - n2, 1), toks, 2 * fc), BF),
             vm((slots, half, 3 * fc), BF),
             vm((half, 3 * fc), BF),
             vm((half, 3 * fc), BF),
@@ -2112,18 +2166,17 @@
     home = (lax.axis_index("batch") * lax.axis_size("z") + z_i) * 2 + x_i
     per_home = HEAD_SIZE // homes
 
-    def spot(value, count):
-        out = jnp.zeros((value.shape[0], homes, count), BF)
-        return lax.dynamic_update_slice(out, value[:, None, :], (0, home, 0)).reshape(-1)
+    def spot(value):
+        here = jnp.arange(homes, dtype=jnp.int32)[None, :, None] == home
+        return jnp.where(here, value[:, None, :], 0).reshape(-1)
 
     biases = jnp.concatenate([b_query, key_bias_rows, value_bias_rows], axis=0)
     small = jnp.concatenate(
-        [spot(biases, per_home), spot(norm_attn[None], rows), spot(norm_mlp[None], rows)]
+        [spot(biases), spot(norm_attn[None]), spot(norm_mlp[None])]
     ).reshape(16, -1)
-    w_qkv = jnp.concatenate([w_query, key_weight_matrix, value_weight_matrix], axis=1)
 
     zs = lax.axis_size("z")
-    n1, n2 = (zs, nc - zs + 1) if rows % 16 == 0 and 2 * zs < nc else (0, nc)
+    n1, n2 = (zs, nc - zs) if rows % 16 == 0 and 2 * zs < nc else (0, nc)
     three = (w_gate, w_up, w_down.T)
     skip = 2 * ffh - ff
 
@@ -2143,7 +2196,8 @@
         lse,
         mid,
         vec,
-        wqkv,
+        wkv,
+        wq,
         wo_t,
         kv_all,
         h2,
@@ -2156,7 +2210,8 @@
         skip,
         fc,
         x_in,
-        w_qkv,
+        jnp.concatenate([key_weight_matrix, value_weight_matrix], axis=1),
+        w_query,
         w_out.T,
         small,
         cos2,
@@ -2191,19 +2246,18 @@
         zs,
         heads,
         left,
-        (y_sum, mlp_g),
+        (y_sum, mlp_g, x_in, cotangent[0]),
         (
             dh2,
             mid,
             vec,
-            x_in,
-            cotangent[0],
             h_first,
             q_mat,
             out_low,
             lse[:, None],
             kv_all,
-            wqkv,
+            wkv,
+            wq,
             wo_t,
             cos2,
             sin2,

time: 482 us -> 474 us (0.983)
  the two profiles are of different devices: /device:TPU:24 before, /device:TPU:8 now
where the time goes in v2:
time: 474 us; the launch traced here: 464 us
  Pallas kernels  456 us (96%)
    pallas_call x1, Pallas kernels, mlp_call(): pl.pallas_call(functools.partial(mlp_kernel, zs, nc, n1, n2, fc, skip), o...  195 us
    pallas_call x1, Pallas kernels, backward_call(): pl.pallas_call(functools.partial(backward_kernel, zs, heads, nl, HEAD_SIZ...  135 us
    pallas_call x1, Pallas kernels, forward_call(): pl.pallas_call(functools.partial(forward_kernel, zs, heads, n1, skip, HEA...  119 us

profile of v2, /device:TPU:8, one launch (start us, length us, event | category | flops | bytes accessed | tf_op | source)
XLA Modules:
  0.0 464.4 jit_solution(5139118057975441080)
XLA Ops:
  0.6 0.0 copy-start.7
  0.7 0.0 copy-start.8
  0.7 0.0 copy-start.6
  0.7 0.0 copy-start.10
  0.7 0.0 copy-start.9
  0.7 0.0 copy-start.2
  0.7 0.0 copy-start.1
  0.8 0.8 reduce-window.4
  1.6 0.7 fusion.8
  2.2 0.1 select_reduce_fusion
  2.3 0.0 copy-start.4
  2.4 1.0 fusion
  3.4 1.0 pad_maximum_fusion
  4.4 0.1 broadcast_in_dim.88
  4.5 0.1 broadcast_in_dim.89
  4.6 0.0 copy-done.7
  4.6 0.1 broadcast_in_dim.91
  4.7 0.0 copy-done.8
  4.7 0.1 broadcast_in_dim.94
  4.8 0.0 copy-done.6
  4.8 0.0 copy-done.10
  4.8 0.0 copy-done.9
  4.8 0.1 broadcast_select_fusion
  4.9 0.1 select_n.89
  5.0 0.6 reshape.180.small_in
  5.6 0.0 copy-done.2
  5.6 0.0 copy-done.1
  5.6 0.6 pad_maximum_fusion.2.wkv_in
  6.2 0.0 copy-done.4
  6.2 118.7 %shard_map.254 = (bf16[512,1536]{1,0:T(8,128)(2,1)}, bf16[512,768]{1,0:T(8,128)(2,1)}, bf16[512,768]{1,0:T(8,128)(2,1)}, f32[2,1536]{1,0:T(2,128)}, f32[256,1536...) custom-call(bf16[512,1536]{1,0:T(8,128)(2,1)} %bitcast.38, ...), custom_call_target="tpu_custom_call" | custom-call | flops 4966055936 | bytes 33554432 | tf_op jit(solution)/shard_map/pallas_call | solution.py:623
  125.0 0.0 copy-start.3
  125.0 195.1 %shard_map.255 = (f32[256,1536]{1,0:T(8,128)}, bf16[4,256,1536]{2,1,0:T(8,128)(2,1)}, bf16[5,192,768]{2,1,0:T(8,128)(2,1)}, bf16[5,1536,768]{2,1,0:T(8,128)(2,1)...) custom-call(bf16[96,4480]{1,0:T(8,128)(2,1)} %refs_0_.3, ...), custom_call_target="tpu_custom_call" | custom-call | flops 65229815808 | bytes 83886080 | tf_op jit(solution)/shard_map/pallas_call | solution.py:2021
  320.1 0.0 copy-done.3
  320.2 0.6 broadcast_in_dim.97.refs_11_
  320.8 134.7 %shard_map.256 = (bf16[2,256,1536]{2,1,0:T(8,128)(2,1)}, bf16[2,256,1536]{2,1,0:T(8,128)(2,1)}, bf16[96,768]{1,0:T(8,128)(2,1)}, bf16[96,256]{1,0:T(8,128)(2,1)}...) custom-call(bf16[4,256,1536]{2,1,0:T(8,128)(2,1)} %get-tuple-element.5, ...), custom_call_target="tpu_custom_call" | custom-call | flops 9932111872 | bytes 33554432 | tf_op jit(solution)/shard_map/pallas_call | solution.py:1426
  455.5 0.0 copy-start
  455.5 7.1 %shard_map.257 = (f32[512,1536]{1,0:T(8,128)}, f32[96,768]{1,0:T(8,128)}, f32[96,128]{1,0:T(8,128)}, f32[96,128]{1,0:T(8,128)}, f32[96,768]{1,0:T(8,128)}, /*ind...) custom-call(bf16[5,2,96,768]{3,2,1,0:T(8,128)(2,1)} %bitcast.31, ...), custom_call_target="tpu_custom_call" | custom-call | tf_op jit(solution)/shard_map/pallas_call | solution.py:2121
  462.6 0.0 copy-done
  462.7 0.1 constant_dynamic-slice_fusion
  462.8 0.5 slice_bitcast_fusion
  463.3 0.1 constant_dynamic-slice_fusion.1
  463.4 0.0 copy-start.5
  463.4 0.5 fusion.9
  463.9 0.1 copy-done.5
  (13 shorter events, 0.1 us)
Async XLA Ops:
  0.6 3.9 copy-start.7
  0.7 4.0 copy-start.8
  0.7 4.1 copy-start.6
  0.7 4.1 copy-start.10
  0.7 4.1 copy-start.9
  0.7 4.9 %copy-start.2 = (bf16[96,128]{1,0:T(8,128)(2,1)S(1)}, bf16[96,128]{1,0:T(8,128)(2,1)}, u32[]{:S(2)}) copy-start(bf16[96,128]{1,0:T(8,128)(2,1)} %param.19) | copy-start | bytes 73732
  0.7 4.9 %copy-start.1 = (bf16[96,128]{1,0:T(8,128)(2,1)S(1)}, bf16[96,128]{1,0:T(8,128)(2,1)}, u32[]{:S(2)}) copy-start(bf16[96,128]{1,0:T(8,128)(2,1)} %param.20) | copy-start | bytes 73732
  2.3 3.9 copy-start.4
  125.0 195.2 %copy-start.3 = (f32[2,1536]{1,0:T(2,128)S(1)}, f32[2,1536]{1,0:T(2,128)}, u32[]{:S(2)}) copy-start(f32[2,1536]{1,0:T(2,128)} %get-tuple-element.60) | copy-start | bytes 36868
  455.5 7.2 %copy-start = (f32[16,256]{1,0:T(8,128)S(1)}, f32[16,256]{1,0:T(8,128)}, u32[]{:S(2)}) copy-start(f32[16,256]{1,0:T(8,128)} %get-tuple-element.74) | copy-start | bytes 49156
  463.4 0.6 copy-start.5

commit v3 on v2

--- a/solution.py
+++ b/solution.py
@@ -1806,7 +1806,7 @@
     b, z, x = lax.axis_index("batch"), lax.axis_index("z"), lax.axis_index("x")
     greet(z, zs)
     rest = nc - n1
-    lag = 0 if n1 else zs
+    lag = 0 if n1 else zs + 1
     ahead = n1 - zs + 1 if n1 else 0
     gather = Gather(zs, mine, full, sems[:6])
     reduce = Reduce(
@@ -1912,6 +1912,13 @@
                 for c in range(rest):
                     trade.sent(c, c)
 
+        c = t - lag
+
+        @pl.when(in_range(c, nc))
+        def _():
+            weights(n1).wait()
+            compute(c)
+
         g = t + ahead
         begin(g)
         for k in range(1, zs):
@@ -1923,11 +1930,17 @@
         @pl.when(in_range(g - zs, rest))
         def _():
             gather.finish(g - zs)
-
-        c = t - lag
-        c_dn = c - 1 - 2 * (zs - 1 - z)
-        c_up = c - 1 - 2 * z
-        c_end = c - 2 * zs
+            weights(g - zs + n1).start()
+
+        if n1:
+
+            @pl.when(c + 1 < n1)
+            def _():
+                weights_one(c + 1).start()
+
+        c_dn = c - 1 - 3 * (zs - 1 - z)
+        c_up = c - 1 - 3 * z
+        c_end = c - 3 * zs + 1
 
         def product_at(step):
             late = step - nl
@@ -1936,17 +1949,6 @@
             )
 
         c_sib = product_at(c - 1)
-
-        @pl.when(in_range(c - n1, rest))
-        def _():
-            weights(c).start()
-
-        if n1:
-
-            @pl.when((c > 0) & (c < n1))
-            def _():
-                weights_one(c).start()
-
         reduce.arrive(c_sib, c_dn, c_up, nc)
         reduce.pass_on(c_sib, c_dn, c_up, nc)
 
@@ -1954,11 +1956,6 @@
         def _():
             reduce.finish(c_end)
             reduce.result(c_end).wait()
-
-        @pl.when(in_range(c, nc))
-        def _():
-            weights(n1).wait()
-            compute(c)
 
         c_prod = product_at(c)
 
@@ -1972,7 +1969,7 @@
         begin(i)
     lax.fori_loop(0, nc + lag, tick, 0)
 
-    end = max(nc + nl + 1, n2 + 2 * zs) + lag
+    end = max(nc + nl + 1, n2 + 3 * zs - 1) + lag
     turn = min(nc + lag + 3, end)
     lax.fori_loop(nc + lag, turn, tick, 0)
     square.turn()

time: 474 us -> 459 us (0.968)
  Pallas kernels: 456 us -> 441 us
    pallas_call x1, Pallas kernels: 195 us -> 181 us  [mlp_call(): pl.pallas_call(functools.partial(mlp_kernel, zs, nc, n1, n2, fc, skip), o...]
where the time goes in v3:
time: 459 us; the launch traced here: 450 us
  Pallas kernels  441 us (96%)
    pallas_call x1, Pallas kernels, mlp_call(): pl.pallas_call(functools.partial(mlp_kernel, zs, nc, n1, n2, fc, skip), o...  181 us
    pallas_call x1, Pallas kernels, backward_call(): pl.pallas_call(functools.partial(backward_kernel, zs, heads, nl, HEAD_SIZ...  135 us
    pallas_call x1, Pallas kernels, forward_call(): pl.pallas_call(functools.partial(forward_kernel, zs, heads, n1, skip, HEA...  119 us

profile of v3, /device:TPU:8, one launch (start us, length us, event | category | flops | bytes accessed | tf_op | source)
XLA Modules:
  0.0 450.1 jit_solution(10983483819177833384)
XLA Ops:
  0.6 0.0 copy-start.7
  0.7 0.0 copy-start.8
  0.7 0.0 copy-start.6
  0.7 0.0 copy-start.10
  0.7 0.0 copy-start.9
  0.7 0.0 copy-start.2
  0.7 0.0 copy-start.1
  0.8 0.8 reduce-window.4
  1.6 0.7 fusion.8
  2.2 0.1 select_reduce_fusion
  2.3 0.0 copy-start.4
  2.4 1.0 fusion
  3.4 1.0 pad_maximum_fusion
  4.4 0.1 broadcast_in_dim.88
  4.5 0.1 broadcast_in_dim.89
  4.6 0.0 copy-done.7
  4.6 0.1 broadcast_in_dim.91
  4.7 0.0 copy-done.8
  4.7 0.1 broadcast_in_dim.94
  4.8 0.0 copy-done.6
  4.8 0.0 copy-done.10
  4.8 0.0 copy-done.9
  4.8 0.1 broadcast_select_fusion
  4.9 0.1 select_n.89
  5.0 0.6 reshape.180.small_in
  5.6 0.0 copy-done.2
  5.6 0.0 copy-done.1
  5.6 0.6 pad_maximum_fusion.2.wkv_in
  6.2 0.0 copy-done.4
  6.2 118.7 %shard_map.254 = (bf16[512,1536]{1,0:T(8,128)(2,1)}, bf16[512,768]{1,0:T(8,128)(2,1)}, bf16[512,768]{1,0:T(8,128)(2,1)}, f32[2,1536]{1,0:T(2,128)}, f32[256,1536...) custom-call(bf16[512,1536]{1,0:T(8,128)(2,1)} %bitcast.38, ...), custom_call_target="tpu_custom_call" | custom-call | flops 4966055936 | bytes 33554432 | tf_op jit(solution)/shard_map/pallas_call | solution.py:623
  125.0 0.0 copy-start.3
  125.0 180.7 %shard_map.255 = (f32[256,1536]{1,0:T(8,128)}, bf16[4,256,1536]{2,1,0:T(8,128)(2,1)}, bf16[5,192,768]{2,1,0:T(8,128)(2,1)}, bf16[5,1536,768]{2,1,0:T(8,128)(2,1)...) custom-call(bf16[96,4480]{1,0:T(8,128)(2,1)} %refs_0_.3, ...), custom_call_target="tpu_custom_call" | custom-call | flops 65229815808 | bytes 83886080 | tf_op jit(solution)/shard_map/pallas_call | solution.py:2018
  305.7 0.0 copy-done.3
  305.7 0.6 broadcast_in_dim.97.refs_11_
  306.3 134.8 %shard_map.256 = (bf16[2,256,1536]{2,1,0:T(8,128)(2,1)}, bf16[2,256,1536]{2,1,0:T(8,128)(2,1)}, bf16[96,768]{1,0:T(8,128)(2,1)}, bf16[96,256]{1,0:T(8,128)(2,1)}...) custom-call(bf16[4,256,1536]{2,1,0:T(8,128)(2,1)} %get-tuple-element.5, ...), custom_call_target="tpu_custom_call" | custom-call | flops 9932111872 | bytes 33554432 | tf_op jit(solution)/shard_map/pallas_call | solution.py:1426
  441.1 0.0 copy-start
  441.1 7.1 %shard_map.257 = (f32[512,1536]{1,0:T(8,128)}, f32[96,768]{1,0:T(8,128)}, f32[96,128]{1,0:T(8,128)}, f32[96,128]{1,0:T(8,128)}, f32[96,768]{1,0:T(8,128)}, /*ind...) custom-call(bf16[5,2,96,768]{3,2,1,0:T(8,128)(2,1)} %bitcast.31, ...), custom_call_target="tpu_custom_call" | custom-call | tf_op jit(solution)/shard_map/pallas_call | solution.py:2118
  448.3 0.0 copy-done
  448.3 0.1 constant_dynamic-slice_fusion
  448.4 0.5 slice_bitcast_fusion
  448.9 0.1 constant_dynamic-slice_fusion.1
  449.0 0.0 copy-start.5
  449.0 0.5 fusion.9
  449.5 0.1 copy-done.5
  (13 shorter events, 0.1 us)
Async XLA Ops:
  0.6 3.9 copy-start.7
  0.7 4.0 copy-start.8
  0.7 4.1 copy-start.6
  0.7 4.1 copy-start.10
  0.7 4.1 copy-start.9
  0.7 4.9 %copy-start.2 = (bf16[96,128]{1,0:T(8,128)(2,1)S(1)}, bf16[96,128]{1,0:T(8,128)(2,1)}, u32[]{:S(2)}) copy-start(bf16[96,128]{1,0:T(8,128)(2,1)} %param.19) | copy-start | bytes 73732
  0.7 4.9 %copy-start.1 = (bf16[96,128]{1,0:T(8,128)(2,1)S(1)}, bf16[96,128]{1,0:T(8,128)(2,1)}, u32[]{:S(2)}) copy-start(bf16[96,128]{1,0:T(8,128)(2,1)} %param.20) | copy-start | bytes 73732
  2.3 3.9 copy-start.4
  125.0 180.7 %copy-start.3 = (f32[2,1536]{1,0:T(2,128)S(1)}, f32[2,1536]{1,0:T(2,128)}, u32[]{:S(2)}) copy-start(f32[2,1536]{1,0:T(2,128)} %get-tuple-element.60) | copy-start | bytes 36868
  441.1 7.2 %copy-start = (f32[16,256]{1,0:T(8,128)S(1)}, f32[16,256]{1,0:T(8,128)}, u32[]{:S(2)}) copy-start(f32[16,256]{1,0:T(8,128)} %get-tuple-element.74) | copy-start | bytes 49156
  449.0 0.6 copy-start.5
